TPU v7x, 512 devices: a whole 4x4x16 slice. The times are simulated.
512 devices in a mesh: ctx: 64 (over y, z), exp: 8 (over x, core).
Axes of the slice: x: 4, y: 4, z: 16, core: 2. Of those that a mesh axis runs over, the one named last changes fastest.
Arguments:
- x_resid: bfloat16 [512, 6144], P('exp', 'ctx'), may hold values from -16 to 16
- queries: bfloat16 [512, 6144], P('ctx', 'exp'), may hold values from -5 to 5
- keys: bfloat16 [32768, 1024], P('ctx', 'exp'), may hold values from -4 to 4
- values: bfloat16 [32768, 1024], P('ctx', 'exp'), may hold values from -4 to 4
- pattern: int32 [4, 6], replicated, may hold values from 0 to 254, as said below
- global_blocks: int32 [2], replicated, may hold values from 0 to 248, as said below
- out_weight: bfloat16 [6144, 6144], P('exp', 'ctx'), may hold values from -0.875 to 0.875
- norm_gain: float32 [6144], P('ctx'), may hold values from 0.1 to 1.9
- router: bfloat16 [6144, 8], P('ctx'), may hold values from -0.078125 to 0.078125
- expert_ids: int32 [512, 2], P('exp'), may hold values from 0 to 7, as said below
- expert_slots: int32 [512, 2], P('exp'), may hold values from 0 to 19, as said below
- w_gate: bfloat16 [8, 6144, 8192], P('exp', None, 'ctx'), may hold values from -0.078125 to 0.078125
- w_up: bfloat16 [8, 6144, 8192], P('exp', None, 'ctx'), may hold values from -0.078125 to 0.078125
- w_down: bfloat16 [8, 8192, 6144], P('exp', None, 'ctx'), may hold values from -0.0625 to 0.0625
Outputs:
- layer_out: bfloat16 [512, 6144], P('exp', 'ctx')
Inputs may be any that keep to these rules, and one draw needn't show every extreme that they name: `pattern`: each row lists 3 + 3 different key blocks, none of them a global block. `global_blocks`: 2 different key blocks. `expert_ids`: each token names two different experts; among the tokens of one index of exp (aligned blocks of 64 rows) every expert is named at most 20 times, and one expert, the same in every block, exactly 20 times. `expert_slots`: within one aligned block of 64 rows, the choices that name the same expert have different slots.
All inputs are finite; a program needn't handle non-finite values.
Results may differ from a plain program's by a relative error of at most 0.01.
Values may be sent and summed in bfloat16 or wider, within the bound.
No kernel may reach another device: no remote copies, remote signals or barrier semaphores. Data moves between devices by JAX's collectives and lax.ppermute only.
A program may use at most 64 MiB of HBM per device.

v0:
```python
import jax
import jax.numpy as jnp
from jax import lax
from jax.sharding import PartitionSpec as P

D = 6144
HD = 128
BLK = 128
CAP = 20


eps = 1e-05
masked_score = -1e30


def per_device(
    x_resid,
    queries,
    keys,
    values,
    pattern,
    global_blocks,
    out_weight,
    norm_gain,
    router,
    expert_ids,
    expert_slots,
    w_gate,
    w_up,
    w_down,
):
    all_queries = lax.all_gather(queries, "ctx", axis=0, tiled=True)
    token_count = all_queries.shape[0]
    cache_length = keys.shape[0]
    groups_local = keys.shape[1] // HD
    group = all_queries.shape[1] // HD // groups_local
    query_heads = all_queries.reshape(token_count, groups_local, group, HD)
    key_heads = keys.reshape(cache_length, groups_local, HD)
    value_heads = values.reshape(cache_length, groups_local, HD)
    scores = jnp.einsum(
        "tkgd,pkd->tkgp", query_heads, key_heads, preferred_element_type=jnp.float32
    ) * HD ** (-0.5)
    local_blocks = cache_length // BLK
    block_ids = lax.axis_index("ctx") * local_blocks + jnp.arange(local_blocks, dtype=jnp.int32)
    listed = jnp.any(pattern[:, :, None] == block_ids[None, None, :], axis=1)
    anchored = jnp.any(global_blocks[:, None] == block_ids[None, :], axis=0)
    allowed_blocks = listed | anchored[None, :]
    allowed = jnp.repeat(jnp.repeat(allowed_blocks, BLK, axis=0), BLK, axis=1)[:, None, None, :]
    local_peak = jnp.max(jnp.where(allowed, scores, masked_score), axis=-1)
    peak = lax.pmax(local_peak, "ctx")
    probs = jnp.where(allowed, jnp.exp(scores - peak[..., None]), 0.0).astype(jnp.bfloat16)
    numerator = jnp.einsum("tkgp,pkd->tkgd", probs, value_heads, preferred_element_type=jnp.float32)
    denominator = jnp.sum(probs, axis=-1, dtype=jnp.float32)
    numerator, denominator = lax.psum((numerator, denominator), "ctx")
    attention = (numerator / denominator[..., None]).astype(jnp.bfloat16).reshape(token_count, -1)
    exp_count = lax.axis_size("exp")
    head_total = lax.psum_scatter(
        jnp.dot(attention, out_weight, preferred_element_type=jnp.float32),
        "exp",
        scatter_dimension=0,
        tiled=True,
    )
    residual = x_resid.astype(jnp.float32) + head_total
    scaled = residual * norm_gain
    router_wide = router.astype(jnp.float32)
    squares = lax.psum(jnp.sum(residual * residual, axis=1), "ctx")
    inverse = lax.rsqrt(squares / D + eps)
    logits = lax.psum(
        jnp.dot(scaled * inverse[:, None], router_wide, precision=lax.Precision.HIGHEST), "ctx"
    )
    normed = (scaled * inverse[:, None]).astype(jnp.bfloat16)
    experts_all = router.shape[1]
    onehot = expert_ids[:, :, None] == jnp.arange(experts_all, dtype=jnp.int32)[None, None, :]
    chosen_logits = jnp.sum(jnp.where(onehot, logits[:, None, :], 0.0), axis=-1)
    gate_weights = jax.nn.sigmoid(chosen_logits - chosen_logits[:, ::-1])
    flat_slots = expert_ids * CAP + expert_slots
    positions = jnp.arange(experts_all * CAP, dtype=jnp.int32)
    dispatch = jnp.sum(
        (flat_slots[None, :, :] == positions[:, None, None]).astype(jnp.bfloat16), axis=2
    )
    local_experts = w_gate.shape[0]
    feature_rows = lax.all_gather(normed, "ctx", axis=1, tiled=True)
    outgoing = jnp.dot(dispatch, feature_rows, preferred_element_type=jnp.float32).astype(
        jnp.bfloat16
    )
    outgoing = outgoing.reshape(experts_all, CAP, -1)
    incoming = lax.all_to_all(outgoing, "exp", split_axis=0, concat_axis=0, tiled=True)
    incoming = incoming.reshape(exp_count, local_experts, CAP, -1)
    expert_gate = jnp.einsum("sjcd,jdf->sjcf", incoming, w_gate, preferred_element_type=jnp.float32)
    expert_lift = jnp.einsum("sjcd,jdf->sjcf", incoming, w_up, preferred_element_type=jnp.float32)
    hidden = (jax.nn.silu(expert_gate) * expert_lift).astype(jnp.bfloat16)
    out_width = w_down.shape[2]
    expert_out = jnp.einsum(
        "sjcf,jfd->sjcd",
        lax.all_gather(hidden, "ctx", axis=3, tiled=True),
        w_down,
        preferred_element_type=jnp.float32,
    ).astype(jnp.bfloat16)
    returned = lax.all_to_all(
        expert_out.reshape(experts_all, CAP, out_width),
        "exp",
        split_axis=0,
        concat_axis=0,
        tiled=True,
    )
    picked = jnp.take(returned.reshape(experts_all * CAP, out_width), flat_slots, axis=0).astype(
        jnp.float32
    )
    mixture = jnp.sum(gate_weights[:, :, None] * picked, axis=1)
    return (residual + mixture).astype(jnp.bfloat16)


def solution(mesh):
    in_specs = (
        P("exp", "ctx"),
        P("ctx", "exp"),
        P("ctx", "exp"),
        P("ctx", "exp"),
        P(),
        P(),
        P("exp", "ctx"),
        P("ctx"),
        P("ctx", None),
        P("exp", None),
        P("exp", None),
        P("exp", None, "ctx"),
        P("exp", None, "ctx"),
        P("exp", None, "ctx"),
    )
    out_specs = P("exp", "ctx")
    return jax.shard_map(
        per_device, mesh=mesh, in_specs=in_specs, out_specs=out_specs, check_vma=False
    )
```

profile of v0, /device:TPU:1, one launch (start us, length us, event | category | flops | bytes accessed | tf_op | source)
XLA Modules:
  0.0 1161.9 jit_solution(5624072325766790315)
XLA Ops:
  6.5 1.0 compare_reduce_fusion
  7.6 0.8 compare_reduce_fusion.1
  8.3 0.1 copy.41
  8.4 0.1 broadcast_bitcast_fusion
  8.5 82.7 %all_gather.9 = bf16[512,768]{1,0:T(8,128)(2,1)S(1)} all-gather(bf16[8,768]{1,0:T(8,128)(2,1)} %param.15), channel_id=1, replica_groups=mesh['ctx'=64,'exp'=8] {'ctx'}, dimensions={0}, use_global_device_ids=true | all-gather | bytes 798720 | tf_op jit(solution)/shard_map/all_gather | solution.py:32
  91.3 0.3 copy.42
  91.5 0.1 broadcast_in_dim.67
  91.6 4.8 fusion
  96.4 221.4 %pmax.7 = f32[512,6]{0,1:T(8,128)S(1)} all-reduce(f32[512,6]{0,1:T(8,128)S(1)} %get-tuple-element.7), channel_id=1, replica_groups=mesh['ctx'=64,'exp'=8] {'ctx'}, use_global_device_ids=true, to_apply=%region_3.4 | all-reduce | flops 3072 | bytes 24576 | tf_op jit(solution)/shard_map/pmax | solution.py:50
  317.8 5.6 fusion.13
  323.4 0.0 all-reduce.2.cloned.1.call-update
  323.4 0.0 reduce-scatter.2.cloned.1.call-start
  323.5 4.1 convert_reduce_fusion
  327.6 219.7 %psum.29 = f32[512,6]{0,1:T(8,128)S(1)} all-reduce(f32[512,6]{0,1:T(8,128)S(1)} %convert_reduce_fusion), channel_id=1, replica_groups=mesh['ctx'=64,'exp'=8] {'ctx'}, use_global_device_ids=true, to_apply=%region_6.7 | all-reduce | flops 3072 | bytes 24576 | tf_op jit(solution)/shard_map/psum | solution.py:54
  547.3 113.2 %all-reduce.2.cloned.1.call-done = f32[512,1,6,128]{3,0,2,1:T(8,128)} async-done(((f32[512,1,6,128]{3,0,2,1:T(8,128)}), f32[512,1,6,128]{3,0,2,1:T(8,128)}) %all-reduce.2.cloned.1.call-update) | async-done | bytes 1572880 | tf_op jit(solution)/shard_map/psum | solution.py:54
  660.5 1.9 divide_convert_fusion
  662.4 0.3 copy.45
  662.7 1.1 fusion.44
  663.8 0.0 all-gather.3.cloned.1.call-start
  663.9 0.6 compare_and_fusion
  664.5 0.6 copy-done.6
  665.0 0.7 fusion.37
  665.7 45.5 %reduce-scatter.2.cloned.1.call-done = f32[64,96]{1,0:T(8,128)} async-done(((f32[512,96]{1,0:T(8,128)}), f32[64,96]{1,0:T(8,128)}) %reduce-scatter.2.cloned.1.call-update) | async-done | bytes 24592 | tf_op jit(solution)/shard_map/reduce_scatter | solution.py:57
  711.2 0.9 multiply_reduce_fusion.1
  712.1 115.6 %psum.30 = f32[64]{0:T(128)S(1)} all-reduce(f32[64]{0:T(128)S(1)} %multiply_reduce_fusion.1), channel_id=1, replica_groups=mesh['ctx'=64,'exp'=8] {'ctx'}, use_global_device_ids=true, to_apply=%region_9.10 | all-reduce | flops 64 | bytes 512 | tf_op jit(solution)/shard_map/psum | solution.py:66
  827.7 0.8 fusion.40
  828.5 72.3 %all-gather = bf16[64,96,64]{1,2,0:T(8,128)(2,1)S(1)} all-gather(bf16[1,96,64]{1,2,0:T(8,128)(2,1)S(1)} %fusion.40), channel_id=1, replica_groups=mesh['ctx'=64,'exp'=8] {'ctx'}, dimensions={0}, use_global_device_ids=true | all-gather | bytes 798720 | tf_op jit(solution)/shard_map/all_gather | solution.py:82
  900.8 0.7 copy.48
  901.5 2.3 reshape.108
  903.8 1.8 convolution_convert_fusion
  905.7 2.1 reshape.89
  907.8 88.6 %all_to_all.10 = bf16[8,20,6144]{2,1,0:T(8,128)(2,1)S(1)} all-to-all(bf16[8,20,6144]{2,1,0:T(8,128)(2,1)} %reshape.89), channel_id=1, replica_groups=mesh['ctx'=64,'exp'=8] {'exp'}, dimensions={0} | all-to-all | bytes 3932160 | tf_op jit(solution)/shard_map/all_to_all | solution.py:87
  996.5 0.8 fusion.16
  997.3 0.6 copy-done.1
  997.8 1.4 fusion.25
  999.3 0.1 copy.49
  999.4 0.1 reshape.99
  999.5 0.1 copy.47
  999.7 0.2 fusion.39
  999.9 113.2 %psum.31 = f32[64,8]{0,1:T(8,128)S(1)} all-reduce(f32[64,8]{0,1:T(8,128)S(1)} %fusion.39), channel_id=1, replica_groups=mesh['ctx'=64,'exp'=8] {'ctx'}, use_global_device_ids=true, to_apply=%region_10.11 | all-reduce | flops 512 | bytes 4096 | tf_op jit(solution)/shard_map/psum | solution.py:68
  1113.1 9.4 all-gather.3.cloned.1.call-done
  1122.6 3.5 fusion.28
  1126.1 22.9 %all-to-all-start.1 = ((bf16[8,20,96]{2,1,0:T(8,128)(2,1)}), bf16[8,20,96]{2,1,0:T(8,128)(2,1)S(1)}, u32[]{:S(2)}, u32[]{:S(2)}) async-start(bf16[8,20,96]{2,1,0:T(8,128)(2,1)} %fusion.28), calls=%async_computation.2 | async-start | bytes 98304 | tf_op jit(solution)/shard_map/all_to_all | solution.py:99
  1149.0 0.1 copy.46
  1149.1 4.7 all-to-all-done.1
  1153.8 0.7 gather_fusion
  1154.5 0.2 multiply_reduce_fusion
  1154.7 0.6 add_convert_fusion
  (47 shorter events, 0.2 us)
Async XLA Ops:
  6.5 989.9 %copy-start = (bf16[1,6144,128]{2,1,0:T(8,128)(2,1)S(1)}, bf16[1,6144,128]{2,1,0:T(8,128)(2,1)}, u32[]{:S(2)}) copy-start(bf16[1,6144,128]{2,1,0:T(8,128)(2,1)} %param.25) | copy-start | bytes 4718596
  6.5 654.0 %all-reduce.2.cloned.1.call-start = ((), (), s32[]{:S(2)}) async-start(), calls=%async_computation.3 | async-start | bytes 3145728 | tf_op jit(solution)/shard_map/psum | solution.py:54
  91.6 226.1 %copy-start.16 = (bf16[512,128]{1,0:T(8,128)(2,1)S(1)}, bf16[512,128]{1,0:T(8,128)(2,1)}, u32[]{:S(2)}) copy-start(bf16[512,128]{1,0:T(8,128)(2,1)} %param.17) | copy-start | bytes 393220
  323.4 387.8 %reduce-scatter.2.cloned.1.call-start = ((), (), s32[]{:S(2)}) async-start(), calls=%async_computation.4 | async-start | bytes 294912 | tf_op jit(solution)/shard_map/reduce_scatter | solution.py:57
  327.6 335.1 %copy-start.4 = (bf16[768,96]{0,1:T(8,128)(2,1)S(1)}, bf16[768,96]{0,1:T(8,128)(2,1)}, u32[]{:S(2)}) copy-start(bf16[768,96]{0,1:T(8,128)(2,1)} %param.20) | copy-start | bytes 442372
  327.6 336.3 %copy-start.8 = (s32[64,2]{0,1:T(2,128)S(1)}, s32[64,2]{0,1:T(2,128)}, u32[]{:S(2)}) copy-start(s32[64,2]{0,1:T(2,128)} %param.23) | copy-start | bytes 1540
  327.6 336.3 %copy-start.11 = (s32[64,2]{0,1:T(2,128)S(1)}, s32[64,2]{0,1:T(2,128)}, u32[]{:S(2)}) copy-start(s32[64,2]{0,1:T(2,128)} %param.24) | copy-start | bytes 1540
  327.6 383.6 %copy-start.5 = (bf16[64,96]{1,0:T(8,128)(2,1)S(1)}, bf16[64,96]{1,0:T(8,128)(2,1)}, u32[]{:S(2)}) copy-start(bf16[64,96]{1,0:T(8,128)(2,1)} %param.14) | copy-start | bytes 36868
  327.6 500.0 %copy-start.12 = (f32[96]{0:T(128)S(1)}, f32[96]{0:T(128)}, u32[]{:S(2)}) copy-start(f32[96]{0:T(128)} %param.21) | copy-start | bytes 1156
  663.8 458.7 %all-gather.3.cloned.1.call-start = ((), (), s32[]{:S(2)}) async-start(), calls=%async_computation.5 | async-start | bytes 3194880 | tf_op jit(solution)/shard_map/all_gather | solution.py:95
  664.5 0.6 copy-start.6
  827.7 73.8 %copy-start.14 = (f32[64]{0:T(128)}, f32[64]{0:T(128)S(1)}, u32[]{:S(2)}) copy-start(f32[64]{0:T(128)S(1)} %add_rsqrt_fusion) | copy-start | bytes 772
  996.4 1.4 copy-start.1
  996.4 2.8 copy-start.7
  996.4 3.1 copy-start.10
  996.4 3.2 copy-start.3
  996.4 3.2 copy-start.13
  996.5 3.2 copy-start.15
  996.5 3.2 copy-start.17
  997.8 115.3 %copy-start.9 = (s32[64,2]{0,1:T(2,128)S(1)}, s32[64,2]{0,1:T(2,128)}, u32[]{:S(2)}) copy-start(s32[64,2]{0,1:T(2,128)} %param.23) | copy-start | bytes 1540
  997.8 124.7 %copy-start.2 = (bf16[1,8192,96]{1,2,0:T(8,128)(2,1)S(1)}, bf16[1,8192,96]{1,2,0:T(8,128)(2,1)}, u32[]{:S(2)}) copy-start(bf16[1,8192,96]{1,2,0:T(8,128)(2,1)} %param.27) | copy-start | bytes 4718596
  1126.1 27.7 %all-to-all-start.1 = ((bf16[8,20,96]{2,1,0:T(8,128)(2,1)}), bf16[8,20,96]{2,1,0:T(8,128)(2,1)S(1)}, u32[]{:S(2)}, u32[]{:S(2)}) async-start(bf16[8,20,96]{2,1,0:T(8,128)(2,1)} %fusion.28), calls=%async_computation.2 | async-start | bytes 98304 | tf_op jit(solution)/shard_map/all_to_all | solution.py:99
Sparse Core Ops, SparseCore 0:
  323.6 336.9 all-reduce.1
  664.0 47.1 reduce-scatter.1
  999.4 123.1 all-gather.2
where the time goes:
time: 1160 us
  blocking collectives  914 us (79%)
  waiting for transfers between devices  173 us (15%)
  starting transfers between devices  23 us (2%)
  matrix products  19.2 us (2%)
  between operations  13.4 us (1%)
  other arithmetic  11.6 us (1%)
    pmax x1, blocking collectives, per_device(): peak = lax.pmax(local_peak, 'ctx')  221 us
    psum x1, blocking collectives, per_device(): numerator, denominator = lax.psum((numerator, denominator), 'ctx')  220 us
    psum x1, blocking collectives, per_device(): squares = lax.psum(jnp.sum(residual * residual, axis=1), 'ctx')  116 us
    psum x1, blocking collectives, per_device(): lax.psum(jnp.dot(scaled * inverse[:, None], router_wide, precision=lax.Pr...  113 us
    psum x1, waiting for transfers between devices, per_device(): numerator, denominator = lax.psum((numerator, denominator), 'ctx')  113 us
    all_to_all x1, blocking collectives, per_device(): lax.all_to_all(outgoing, 'exp', split_axis=0, concat_axis=0, tiled=True)  88.6 us
    all_gather x1, blocking collectives, per_device(): all_queries = lax.all_gather(queries, 'ctx', axis=0, tiled=True)  82.7 us
    all_gather x1, blocking collectives, per_device(): feature_rows = lax.all_gather(normed, 'ctx', axis=1, tiled=True)  72.3 us
  transfers between devices with their start and end apart: 4, of which 4 were waited for; matrix products, arithmetic and copies ran while one was open for 1% of the time, Pallas kernels for 0%

commit v1 on v0

v1 whole, which is shorter than its diff:
```python
import jax
import jax.numpy as jnp
from jax import lax
from jax.experimental import pallas as pl
from jax.experimental.pallas import tpu as pltpu
from jax.sharding import Mesh, PartitionSpec as P

D = 6144
HD = 128
BLK = 128
CAP = 20
NY, NZ, NE = 4, 16, 8
GROUP = 6
NSEL = 8
FEAT = 96
WIDE = NY * FEAT
TOKB = 128
ROWS = 2 * CAP
FIRST = -1e4
EPS = 1e-05
R_W = FEAT
R_K = R_W + GROUP * FEAT
R_V = R_K + 4 * BLK
R_ALL = R_V + 4 * BLK
L_ROUTER, L_SQ, L_GAIN = 64, 72, 72
BF, F32 = jnp.bfloat16, jnp.float32
NT = (((1,), (1,)), ((), ()))


def call(body, out_shape, n_in, smem=(), scratch=(), blocks=None):
    vmem = pl.BlockSpec(memory_space=pltpu.VMEM)
    specs = [pl.BlockSpec(memory_space=pltpu.SMEM) if i in smem else vmem for i in range(n_in)]
    return pl.pallas_call(
        body,
        out_shape=out_shape,
        in_specs=specs,
        out_specs=jax.tree.map(lambda _: vmem, out_shape),
        scratch_shapes=list(scratch),
        compiler_params=pltpu.CompilerParams(vmem_limit_bytes=48 * 1024 * 1024),
    )


def lanes(rows, width=128):
    return lax.broadcasted_iota(jnp.int32, (rows, width), 1)


def pack_body(k_ref, v_ref, w_ref, xt_ref, r_ref, g_ref, o_ref):
    gain = g_ref[...]
    hi = gain.astype(BF).astype(F32)
    mid = (gain - hi).astype(BF).astype(F32)
    lo = gain - hi - mid
    lane = lanes(FEAT)
    misc = xt_ref[...].astype(F32) + r_ref[...].astype(F32)
    misc = jnp.where(lane == L_GAIN, hi, misc)
    misc = jnp.where(lane == L_GAIN + 1, mid, misc)
    misc = jnp.where(lane == L_GAIN + 2, lo, misc).astype(BF)
    for y in range(NY):
        o_ref[y, 0:FEAT, :] = misc
        for g in range(GROUP):
            o_ref[y, R_W + g * FEAT : R_W + (g + 1) * FEAT, :] = w_ref[:, g * 128 : (g + 1) * 128]
        o_ref[y, R_K : R_K + 512, :] = k_ref[...]
        o_ref[y, R_V : R_V + 512, :] = v_ref[...]


def attend_body(s_ref, kv_ref, q_ref, o_ref, acc_ref, m_ref, l_ref):
    acc_ref[...] = jnp.zeros_like(acc_ref)
    l_ref[...] = jnp.zeros_like(l_ref)
    m_ref[...] = jnp.full(m_ref.shape, FIRST, F32)
    here = s_ref[NSEL]
    for i in range(NSEL):
        block = s_ref[i]
        owner = block >> 2

        @pl.when((owner & (NZ - 1)) == here)
        def _():
            row = owner >> 4
            start = pl.multiple_of((block & 3) * BLK, BLK)
            keys = kv_ref[row, pl.ds(R_K + start, BLK), :]
            values = kv_ref[row, pl.ds(R_V + start, BLK), :]
            query = jnp.concatenate(
                [q_ref[:, g * HD : (g + 1) * HD] for g in range(GROUP)], axis=0
            )
            s = lax.dot_general(query, keys, NT, preferred_element_type=F32) * HD ** (-0.5)
            old = m_ref[...]
            new = jnp.maximum(old, jnp.max(s, axis=1, keepdims=True))
            p = jnp.exp(s - new).astype(BF)
            keep = jnp.exp(old - new)
            l_ref[...] = l_ref[...] * keep + jnp.sum(p.astype(F32), axis=1, keepdims=True)
            acc_ref[...] = acc_ref[...] * keep + jnp.dot(p, values, preferred_element_type=F32)
            m_ref[...] = new

    lane = lanes(TOKB)
    stats = jnp.zeros((TOKB, 128), F32)
    for g in range(GROUP):
        rows = slice(g * TOKB, (g + 1) * TOKB)
        m, l = m_ref[rows, :], l_ref[rows, :]
        o_ref[:, g * HD : (g + 1) * HD] = (acc_ref[rows, :] / jnp.where(l > 0, l, 1.0)).astype(BF)
        near = m.astype(BF).astype(F32)
        total = l * jnp.exp(m - near)
        high = total.astype(BF).astype(F32)
        stats = jnp.where(lane == g, near, stats)
        stats = jnp.where(lane == 8 + g, high, stats)
        stats = jnp.where(lane == 16 + g, total - high, stats)
    o_ref[:, GROUP * HD :] = stats.astype(BF)


def merge_body(r_ref, o_ref):
    got = r_ref[...].astype(F32)
    stats = got[:, :, GROUP * HD :]
    for g in range(GROUP):
        m = stats[:, :, g : g + 1]
        l = stats[:, :, 8 + g : 9 + g] + stats[:, :, 16 + g : 17 + g]
        weight = l * jnp.exp(m - jnp.max(m, axis=0, keepdims=True))
        top = jnp.sum(weight * got[:, :, g * HD : (g + 1) * HD], axis=0)
        out = (top / jnp.sum(weight, axis=0)).astype(BF)
        o_ref[:, :, g * HD : (g + 1) * HD] = jnp.broadcast_to(out[None], (NZ,) + out.shape)


def project_body(s_ref, a_ref, w_ref, id_ref, o_ref):
    y, e = s_ref[0], s_ref[1]
    total = jnp.zeros((TOKB, WIDE), F32)
    for g in range(GROUP):
        w = jnp.concatenate(
            [w_ref[n, R_W + g * FEAT : R_W + (g + 1) * FEAT, :] for n in range(NY)], axis=0
        )
        total += lax.dot_general(
            a_ref[:, g * 128 : (g + 1) * 128], w, NT, preferred_element_type=F32
        )
    misc = jnp.concatenate([w_ref[n, 0:FEAT, :] for n in range(NY)], axis=0)
    row = lax.broadcasted_iota(jnp.int32, (TOKB, 128), 0)
    mine = (row == lanes(TOKB) + (e & 1) * 64) & (lanes(TOKB) < 64) & ((e >> 1) == y)
    total += lax.dot_general(
        jnp.where(mine, 1.0, 0.0).astype(BF), misc, NT, preferred_element_type=F32
    )
    out = total.astype(BF)
    for n in range(NE):
        o_ref[n, 0:TOKB, :] = out
        o_ref[n, TOKB:, :] = id_ref[...]


def pick_body(s_ref, r_ref, w_ref, x_ref, loc_ref):
    y, e = s_ref[0], s_ref[1]
    res = r_ref[0, 0:TOKB, :].astype(F32)
    for n in range(1, NE):
        res += r_ref[n, 0:TOKB, :].astype(F32)
    misc = jnp.concatenate([w_ref[n, 0:FEAT, :] for n in range(NY)], axis=0)
    sub = lax.broadcasted_iota(jnp.int32, (8, 128), 0)
    take = (lanes(8) == L_GAIN + sub) & (sub < 3)
    gain = lax.dot_general(
        jnp.where(take, 1.0, 0.0).astype(BF), misc, NT, preferred_element_type=F32
    )
    gain = jnp.sum(gain, axis=0, keepdims=True)
    scaled = res * gain
    sq = jnp.sum(res * res, axis=1, keepdims=True)
    high = scaled.astype(BF)
    low = (scaled - high.astype(F32)).astype(BF)
    logits = jnp.dot(high, misc, preferred_element_type=F32) + jnp.dot(
        low, misc, preferred_element_type=F32
    )
    lane = lanes(TOKB)
    stats = jnp.where((lane >= L_ROUTER) & (lane < L_ROUTER + 8), logits, 0.0)
    stats = jnp.where(lane == L_SQ, sq, stats)
    stats_high = stats.astype(BF).astype(F32)
    both = (stats_high + pltpu.roll(stats - stats_high, 64, 1)).astype(BF)
    ids = r_ref[2 * y, TOKB:, :].astype(F32) + r_ref[2 * y + 1, TOKB:, :].astype(F32)
    id0, id1 = ids[0:1, 0:128], ids[0:1, 128:256]
    slot0, slot1 = ids[1:2, 0:128], ids[1:2, 128:256]
    want = lax.broadcasted_iota(jnp.int32, (ROWS, 128), 0).astype(F32)
    base = jnp.where(lanes(1) >= 64, float(CAP), 0.0)
    me = e.astype(F32)
    m0 = jnp.where((id0 == me) & (slot0 + base == want), 1.0, 0.0)
    m1 = jnp.where((id1 == me) & (slot1 + base == want), 1.0, 0.0)
    choose = (m0 + m1).astype(BF)
    other = jnp.sum(m0 * id1 + m1 * id0, axis=1, keepdims=True)
    first = jnp.sum(m0, axis=1, keepdims=True)
    x_ref[:, 0:WIDE] = jnp.dot(choose, high, preferred_element_type=F32).astype(BF)
    x_ref[:, WIDE:] = jnp.dot(choose, both, preferred_element_type=F32).astype(BF)
    res_high = res.astype(BF)
    res_low = (res - res_high.astype(F32)).astype(BF)
    loc_ref[:, 0:WIDE] = jnp.dot(choose, res_high, preferred_element_type=F32)
    loc_ref[:, WIDE : 2 * WIDE] = jnp.dot(choose, res_low, preferred_element_type=F32)
    side = lanes(ROWS)
    loc_ref[:, 2 * WIDE :] = jnp.where(side == 0, other, jnp.where(side == 1, first, 0.0))


def norm_body(s_ref, g_ref, loc_ref, o_ref):
    e = s_ref[1]
    stats = g_ref[0, :, WIDE:].astype(F32)
    for z in range(1, NZ):
        stats += g_ref[z, :, WIDE:].astype(F32)
    stats = stats + pltpu.roll(stats, 64, 1)
    inverse = lax.rsqrt(stats[:, L_SQ : L_SQ + 1] / D + EPS)
    other = loc_ref[:, 2 * WIDE : 2 * WIDE + 1]
    first = loc_ref[:, 2 * WIDE + 1 : 2 * WIDE + 2]
    lane = lanes(ROWS)
    mine = jnp.sum(jnp.where(lane == L_ROUTER + e, stats, 0.0), axis=1, keepdims=True)
    rival = jnp.where(lane.astype(F32) == other + float(L_ROUTER), stats, 0.0)
    rival = jnp.sum(rival, axis=1, keepdims=True)
    gate = 1.0 / (1.0 + jnp.exp((rival - mine) * inverse))
    gate_high = gate.astype(BF).astype(F32)
    for z in range(NZ):
        normed = (g_ref[z, :, 0:WIDE].astype(F32) * inverse).astype(BF)
        for n in range(NY):
            o_ref[n, :, z * WIDE : (z + 1) * WIDE] = normed
    zeros = jnp.zeros((ROWS, 128 - FEAT), F32)
    tail = lanes(ROWS, 128 - FEAT)
    for n in range(NY):
        o_ref[n, :, D : D + FEAT] = loc_ref[:, n * FEAT : (n + 1) * FEAT].astype(BF)
        o_ref[n, :, D + 128 : D + 128 + FEAT] = loc_ref[
            :, WIDE + n * FEAT : WIDE + (n + 1) * FEAT
        ].astype(BF)
        o_ref[n, :, D + FEAT : D + 128] = jnp.where(
            tail == 0, gate_high, jnp.where(tail == 1, first, zeros)
        ).astype(BF)
        o_ref[n, :, D + 128 + FEAT :] = jnp.where(tail == 0, gate - gate_high, zeros).astype(BF)


def lift_body(x_ref, wg_ref, wu_ref, o_ref):
    gate = jnp.zeros((NY * ROWS, 128), F32)
    lift = jnp.zeros((NY * ROWS, 128), F32)
    for z in range(NZ):
        x = x_ref[:, z * WIDE : (z + 1) * WIDE]
        wg = jnp.concatenate([wg_ref[n, z] for n in range(NY)], axis=0)
        wu = jnp.concatenate([wu_ref[n, z] for n in range(NY)], axis=0)
        gate += jnp.dot(x, wg, preferred_element_type=F32)
        lift += jnp.dot(x, wu, preferred_element_type=F32)
    o_ref[...] = (gate / (1.0 + jnp.exp(-gate)) * lift).astype(BF)


def down_body(h_ref, w_ref, x_ref, o_ref):
    total = jnp.zeros((NY * ROWS, FEAT), F32)
    for n in range(NY):
        for z in range(0, NZ, 4):
            h = jnp.concatenate([h_ref[n, z + i] for i in range(4)], axis=1)
            at = (n * NZ + z) * 128
            total += lax.dot_general(
                h, w_ref[:, at : at + 512], NT, preferred_element_type=F32
            )
    rounded = total.astype(BF).astype(F32)
    high = x_ref[:, 0:128].astype(F32)
    low = x_ref[:, 128:256].astype(F32)
    gate = high[:, FEAT : FEAT + 1] + low[:, FEAT : FEAT + 1]
    first = high[:, FEAT + 1 : FEAT + 2]
    residual = high[:, 0:FEAT] + low[:, 0:FEAT]
    o_ref[...] = gate * rounded + jnp.where(first > 0.5, residual, 0.0)


def swap(x, axis):
    return lax.all_to_all(x, axis, split_axis=0, concat_axis=0, tiled=True)


def shape(*dims, dtype=BF):
    return jax.ShapeDtypeStruct(dims, dtype)


def per_device(
    x_resid,
    queries,
    keys,
    values,
    pattern,
    global_blocks,
    out_weight,
    norm_gain,
    router,
    expert_ids,
    expert_slots,
    w_gate,
    w_up,
    w_down,
):
    y, z, e = lax.axis_index("y"), lax.axis_index("z"), lax.axis_index("exp")
    place = jnp.stack([y, e]).astype(jnp.int32)
    listed = jnp.concatenate([pattern[y], global_blocks, z[None].astype(jnp.int32)])

    pairs = jnp.concatenate([expert_ids.T, expert_slots.T], axis=0).astype(BF)
    blank = jnp.zeros_like(pairs)
    pairs = jnp.where(
        (e & 1) == 0,
        jnp.concatenate([pairs, blank], axis=1),
        jnp.concatenate([blank, pairs], axis=1),
    )
    id_rows = jnp.pad(pairs.reshape(2, 256), ((0, 14), (0, 128)))

    packed = call(pack_body, shape(NY, R_ALL, 128), 6)(
        keys,
        values,
        out_weight.T,
        jnp.pad(x_resid.T, ((0, 0), (0, 64))),
        jnp.pad(router, ((0, 0), (L_ROUTER, 128 - L_ROUTER - 8))),
        norm_gain[:, None],
    )
    column = swap(packed, "y")
    block_queries = swap(jnp.broadcast_to(queries[None], (NZ,) + queries.shape), "z")

    partial = call(
        attend_body,
        shape(TOKB, (GROUP + 1) * HD),
        3,
        smem=(0,),
        scratch=[pltpu.VMEM((GROUP * TOKB, 128), F32)] * 3,
    )(listed, column, block_queries.reshape(TOKB, GROUP * HD))
    partial = swap(partial.reshape(NZ, TOKB // NZ, (GROUP + 1) * HD), "z")
    attention = call(merge_body, shape(NZ, TOKB // NZ, GROUP * HD), 1)(partial)
    attention = swap(attention, "z").reshape(TOKB, GROUP * HD)

    products = call(project_body, shape(NE, TOKB + 16, WIDE), 4, smem=(0,))(
        place, attention, column[:, :R_K], id_rows
    )
    products = swap(products, "exp")
    rows, local = call(
        pick_body,
        (shape(ROWS, WIDE + 128), shape(ROWS, 2 * WIDE + 128, dtype=F32)),
        3,
        smem=(0,),
    )(place, products, column[:, :R_W])
    gathered = lax.all_gather(rows, "z", axis=0)
    normed = call(norm_body, shape(NY, ROWS, D + 256), 3, smem=(0,))(place, gathered, local)
    normed = swap(normed, "y").reshape(NY * ROWS, D + 256)

    hidden = call(lift_body, shape(NY * ROWS, 128), 3)(
        normed, w_gate.reshape(NY, NZ, FEAT, 128), w_up.reshape(NY, NZ, FEAT, 128)
    )
    hidden = lax.all_gather(hidden, "z", axis=0)
    hidden = swap(jnp.broadcast_to(hidden[None], (NY,) + hidden.shape), "y")
    hidden = hidden.reshape(NY, NZ, NY * ROWS, 128)
    out = call(down_body, shape(NY * ROWS, FEAT, dtype=F32), 3)(
        hidden, w_down[0].T, normed[:, D:]
    )
    back = swap(out.reshape(NE, CAP, FEAT), "exp").reshape(NE * CAP, FEAT)
    flat = expert_ids * CAP + expert_slots
    at = jnp.arange(NE * CAP, dtype=jnp.int32)[None, :]
    both = (flat[:, :1] == at).astype(F32) + (flat[:, 1:] == at).astype(F32)
    return jnp.dot(both, back, precision=lax.Precision.HIGHEST).astype(BF)


def solution(mesh):
    inner = Mesh(mesh.devices.reshape(NY, NZ, NE), ("y", "z", "exp"))
    ctx = ("y", "z")
    in_specs = (
        P("exp", ctx),
        P(ctx, "exp"),
        P(ctx, "exp"),
        P(ctx, "exp"),
        P(),
        P(),
        P("exp", ctx),
        P(ctx),
        P(ctx, None),
        P("exp", None),
        P("exp", None),
        P("exp", None, ctx),
        P("exp", None, ctx),
        P("exp", None, ctx),
    )
    return jax.shard_map(
        per_device, mesh=inner, in_specs=in_specs, out_specs=P("exp", ctx), check_vma=False
    )
```

time: 1160 us -> 252 us (0.22)
  blocking collectives: 914 us -> 96.7 us
  waiting for transfers between devices: 173 us -> 70.5 us
  starting transfers between devices: 23 us -> 61.5 us
  matrix products: 19.2 us -> 0.87 us
  between operations: 13.4 us -> 0.17 us
    psum x3 -> x0, blocking collectives: 449 us -> none  [the longest x1 220 us: per_device(): numerator, denominator = lax.psum((numerator, denominator), 'ctx')]
    pmax x1 -> x0, blocking collectives: 221 us -> none  [per_device(): peak = lax.pmax(local_peak, 'ctx')]
    psum x1 -> x0, waiting for transfers between devices: 113 us -> none  [per_device(): numerator, denominator = lax.psum((numerator, denominator), 'ctx')]
    all_gather x2, blocking collectives: 155 us -> 49.7 us  [the longest x1 26.2 us: per_device(): gathered = lax.all_gather(rows, 'z', axis=0)]
    all_to_all x1 -> x6, waiting for transfers between devices: 4.7 us -> 70.5 us  [swap(): return lax.all_to_all(x, axis, split_axis=0, concat_axis=0, tiled=True)]
    reduce_scatter x1 -> x0, waiting for transfers between devices: 45.5 us -> none  [per_device(): lax.psum_scatter(jnp.dot(attention, out_weight, preferred_element_type=jn...]
    all_to_all x1 -> x2, blocking collectives: 88.6 us -> 47 us  [swap(): return lax.all_to_all(x, axis, split_axis=0, concat_axis=0, tiled=True)]
    all_to_all x1 -> x6, starting transfers between devices: 22.9 us -> 61.5 us  [swap(): return lax.all_to_all(x, axis, split_axis=0, concat_axis=0, tiled=True)]
  transfers between devices with their start and end apart: 4 -> 6, of which waited for: 4 -> 6; matrix products, arithmetic and copies ran while one was open for 1% -> 1% of each run, Pallas kernels for 0% -> 1%
where the time goes in v1:
time: 252 us; the launch traced here: 251 us
  blocking collectives  96.7 us (38%)
  waiting for transfers between devices  70.5 us (28%)
  starting transfers between devices  61.5 us (24%)
  local copies, waits for them, and re-layouts  11.7 us (5%)
  Pallas kernels  9.64 us (4%)
    all_to_all x6, waiting for transfers between devices, swap(): return lax.all_to_all(x, axis, split_axis=0, concat_axis=0, tiled=True)  70.5 us
    all_to_all x6, starting transfers between devices, swap(): return lax.all_to_all(x, axis, split_axis=0, concat_axis=0, tiled=True)  61.5 us
    all_to_all x2, blocking collectives, swap(): return lax.all_to_all(x, axis, split_axis=0, concat_axis=0, tiled=True)  47 us
    all_gather x1, blocking collectives, per_device(): gathered = lax.all_gather(rows, 'z', axis=0)  26.2 us
    all_gather x1, blocking collectives, per_device(): hidden = lax.all_gather(hidden, 'z', axis=0)  23.5 us
    unnamed x24, local copies, waits for them, and re-layouts  5.9 us
  transfers between devices with their start and end apart: 6, of which 6 were waited for; matrix products, arithmetic and copies ran while one was open for 1% of the time, Pallas kernels for 1%

profile of v1, /device:TPU:1, one launch (start us, length us, event | category | flops | bytes accessed | tf_op | source)
XLA Modules:
  0.0 251.3 jit_solution(432246211447034158)
XLA Ops:
  0.0 0.0 copy-start
  0.0 1.4 broadcast_in_dim.10
  1.4 15.7 %all-to-all-start.1 = ((bf16[16,8,768]{2,1,0:T(8,128)(2,1)}), bf16[16,8,768]{2,1,0:T(8,128)(2,1)S(1)}, u32[]{:S(2)}, u32[]{:S(2)}) async-start(bf16[16,8,768]{2,1,0:T(8,128)(2,1)} %broadcast_in_dim.10), calls=%async_computation.1 | async-start | bytes 393216 | tf_op jit(solution)/shard_map/all_to_all | solution.py:249
  17.2 0.8 copy.18
  18.0 0.8 copy.19
  18.8 0.1 pad.15.r_ref
  18.9 0.8 copy.20.g_ref
  19.6 0.9 copy-done.5
  20.5 0.9 copy-done.6
  21.5 0.9 copy-done.7
  22.4 1.4 shard_map.136
  23.8 5.9 %all-to-all-done.1 = bf16[16,8,768]{2,1,0:T(8,128)(2,1)S(1)} async-done(((bf16[16,8,768]{2,1,0:T(8,128)(2,1)}), bf16[16,8,768]{2,1,0:T(8,128)(2,1)S(1)}, u32[]{:S(2)}, u32[]{:S(2)}) %all-to-all-start.1) | async-done | bytes 196640 | tf_op jit(solution)/shard_map/all_to_all | solution.py:249
  29.7 4.2 %all-to-all-start = ((bf16[4,1696,128]{2,1,0:T(8,128)(2,1)}), bf16[4,1696,128]{2,1,0:T(8,128)(2,1)S(1)}, u32[]{:S(2)}, u32[]{:S(2)}) async-start(bf16[4,1696,128]{2,1,0:T(8,128)(2,1)} %shard_map.136), calls=%async_computation | async-start | bytes 3473408 | tf_op jit(solution)/shard_map/all_to_all | solution.py:249
  33.9 0.0 copy-done
  33.9 0.0 copy-done.10
  33.9 0.1 pad_add_fusion.1.s_ref
  34.0 17.0 %all-to-all-done.kv_ref = bf16[4,1696,128]{2,1,0:T(8,128)(2,1)S(1)} async-done(((bf16[4,1696,128]{2,1,0:T(8,128)(2,1)}), bf16[4,1696,128]{2,1,0:T(8,128)(2,1)S(1)}, u32[]{:S(2)}, u32[]{:S(2)}) %all-to-all-start) | async-done | bytes 1736736 | tf_op jit(solution)/shard_map/all_to_all | solution.py:249
  51.0 0.9 shard_map.137
  51.9 26.1 %all_to_all.40.r_ref = bf16[16,8,896]{2,1,0:T(8,128)(2,1)S(1)} all-to-all(bf16[16,8,896]{2,1,0:T(8,128)(2,1)S(1)} %bitcast.34), channel_id=1, replica_groups=mesh['y'=4,'z'=16,'exp'=8] {'z'}, dimensions={0} | all-to-all | bytes 458752 | tf_op jit(solution)/shard_map/all_to_all | solution.py:249
  78.1 1.2 shard_map.138
  79.2 8.7 %all-to-all-start.3 = ((bf16[16,8,768]{2,1,0:T(8,128)(2,1)}), bf16[16,8,768]{2,1,0:T(8,128)(2,1)S(1)}, u32[]{:S(2)}, u32[]{:S(2)}) async-start(bf16[16,8,768]{2,1,0:T(8,128)(2,1)} %shard_map.138), calls=%async_computation.3 | async-start | bytes 393216 | tf_op jit(solution)/shard_map/all_to_all | solution.py:249
  87.9 0.0 copy-done.8
  87.9 0.0 copy-done.9
  88.0 0.1 pad_select_fusion
  88.1 0.1 pad_add_fusion.s_ref
  88.2 12.1 %all-to-all-done.3 = bf16[16,8,768]{2,1,0:T(8,128)(2,1)S(1)} async-done(((bf16[16,8,768]{2,1,0:T(8,128)(2,1)}), bf16[16,8,768]{2,1,0:T(8,128)(2,1)S(1)}, u32[]{:S(2)}, u32[]{:S(2)}) %all-to-all-start.3) | async-done | bytes 196640 | tf_op jit(solution)/shard_map/all_to_all | solution.py:249
  100.2 1.9 shard_map.139
  102.2 9.8 %all-to-all-start.4 = ((bf16[8,144,384]{2,1,0:T(8,128)(2,1)}), bf16[8,144,384]{2,1,0:T(8,128)(2,1)S(1)}, u32[]{:S(2)}, u32[]{:S(2)}) async-start(bf16[8,144,384]{2,1,0:T(8,128)(2,1)} %shard_map.139), calls=%async_computation.4 | async-start | bytes 1769472 | tf_op jit(solution)/shard_map/all_to_all | solution.py:249
  111.9 13.3 %all-to-all-done.4.r_ref = bf16[8,144,384]{2,1,0:T(8,128)(2,1)S(1)} async-done(((bf16[8,144,384]{2,1,0:T(8,128)(2,1)}), bf16[8,144,384]{2,1,0:T(8,128)(2,1)S(1)}, u32[]{:S(2)}, u32[]{:S(2)}) %all-to-all-start.4) | async-done | bytes 884768 | tf_op jit(solution)/shard_map/all_to_all | solution.py:249
  125.3 1.1 shard_map.140
  126.4 26.2 %all-gather = bf16[640,512]{1,0:T(8,128)(2,1)S(1)} all-gather(bf16[40,512]{1,0:T(8,128)(2,1)S(1)} %get-tuple-element.7), channel_id=2, replica_groups=mesh['y'=4,'z'=16,'exp'=8] {'z'}, dimensions={0}, use_global_device_ids=true | all-gather | bytes 696320 | tf_op jit(solution)/shard_map/all_gather | solution.py:317
  152.6 1.0 shard_map.141
  153.7 0.0 copy-start.3
  153.7 0.0 copy-start.4
  153.7 20.8 %all_to_all.41 = bf16[4,40,6400]{2,1,0:T(8,128)(2,1)S(1)} all-to-all(bf16[4,40,6400]{2,1,0:T(8,128)(2,1)S(1)} %shard_map.141), channel_id=1, replica_groups=mesh['y'=4,'z'=16,'exp'=8] {'y'}, dimensions={0} | all-to-all | bytes 4096000 | tf_op jit(solution)/shard_map/all_to_all | solution.py:249
  174.5 1.2 shard_map.142
  175.7 0.1 copy-done.1
  175.9 23.5 %all-gather.1 = bf16[2560,128]{1,0:T(8,128)(2,1)S(1)} all-gather(bf16[160,128]{1,0:T(8,128)(2,1)S(1)} %shard_map.142), channel_id=3, replica_groups=mesh['y'=4,'z'=16,'exp'=8] {'z'}, dimensions={0}, use_global_device_ids=true | all-gather | bytes 696320 | tf_op jit(solution)/shard_map/all_gather | solution.py:324
  199.4 1.9 broadcast_in_dim.11
  201.3 3.7 %all-to-all-start.6 = ((bf16[4,16,160,128]{3,2,1,0:T(8,128)(2,1)}), bf16[4,16,160,128]{3,2,1,0:T(8,128)(2,1)S(1)}, u32[]{:S(2)}, u32[]{:S(2)}) async-start(bf16[4,16,160,128]{3,2,1,0:T(8,128)(2,1)} %broadcast_in_dim.11), calls=%async_computation.6 | async-start | bytes 5242880 | tf_op jit(solution)/shard_map/all_to_all | solution.py:249
  204.9 0.9 slice.22.x_ref
  205.8 17.2 %all-to-all-done.6.h_ref = bf16[4,16,160,128]{3,2,1,0:T(8,128)(2,1)S(1)} async-done(((bf16[4,16,160,128]{3,2,1,0:T(8,128)(2,1)}), bf16[4,16,160,128]{3,2,1,0:T(8,128)(2,1)S(1)}, u32[]{:S(2)}, u32[]{:S(2)}) %all-to-all-start.6) | async-done | bytes 2621472 | tf_op jit(solution)/shard_map/all_to_all | solution.py:249
  223.1 1.4 copy-done.2
  224.5 0.8 shard_map.143
  225.3 0.6 reshape.36
  226.0 19.5 %all-to-all-start.7 = ((f32[8,20,96]{2,1,0:T(8,128)}), f32[8,20,96]{2,1,0:T(8,128)S(1)}, u32[]{:S(2)}, u32[]{:S(2)}) async-start(f32[8,20,96]{2,1,0:T(8,128)} %reshape.36), calls=%async_computation.7 | async-start | bytes 196608 | tf_op jit(solution)/shard_map/all_to_all | solution.py:249
  245.4 5.0 %all-to-all-done.7 = f32[8,20,96]{2,1,0:T(8,128)S(1)} async-done(((f32[8,20,96]{2,1,0:T(8,128)}), f32[8,20,96]{2,1,0:T(8,128)S(1)}, u32[]{:S(2)}, u32[]{:S(2)}) %all-to-all-start.7) | async-done | bytes 61472 | tf_op jit(solution)/shard_map/all_to_all | solution.py:249
  250.4 0.9 convolution_convert_fusion
  (20 shorter events, 0.1 us)
Async XLA Ops:
  0.0 33.9 %copy-start = (s32[4,6]{1,0:T(4,128)S(1)}, s32[4,6]{1,0:T(4,128)}, u32[]{:S(2)}) copy-start(s32[4,6]{1,0:T(4,128)} %param.18) | copy-start | bytes 292
  1.4 28.3 %all-to-all-start.1 = ((bf16[16,8,768]{2,1,0:T(8,128)(2,1)}), bf16[16,8,768]{2,1,0:T(8,128)(2,1)S(1)}, u32[]{:S(2)}, u32[]{:S(2)}) async-start(bf16[16,8,768]{2,1,0:T(8,128)(2,1)} %broadcast_in_dim.10), calls=%async_computation.1 | async-start | bytes 393216 | tf_op jit(solution)/shard_map/all_to_all | solution.py:249
  19.6 0.9 copy-start.5
  20.5 0.9 copy-start.6
  21.4 0.9 copy-start.7
  23.8 10.1 %copy-start.10 = (s32[2]{0:T(128)S(1)}, s32[2]{0:T(128)}, u32[]{:S(2)}) copy-start(s32[2]{0:T(128)} %param.19) | copy-start | bytes 28
  29.7 21.3 %all-to-all-start = ((bf16[4,1696,128]{2,1,0:T(8,128)(2,1)}), bf16[4,1696,128]{2,1,0:T(8,128)(2,1)S(1)}, u32[]{:S(2)}, u32[]{:S(2)}) async-start(bf16[4,1696,128]{2,1,0:T(8,128)(2,1)} %shard_map.136), calls=%async_computation | async-start | bytes 3473408 | tf_op jit(solution)/shard_map/all_to_all | solution.py:249
  33.9 54.0 %copy-start.8 = (s32[64,2]{0,1:T(2,128)S(1)}, s32[64,2]{0,1:T(2,128)}, u32[]{:S(2)}) copy-start(s32[64,2]{0,1:T(2,128)} %param.24) | copy-start | bytes 1540
  33.9 54.0 %copy-start.9 = (s32[64,2]{0,1:T(2,128)S(1)}, s32[64,2]{0,1:T(2,128)}, u32[]{:S(2)}) copy-start(s32[64,2]{0,1:T(2,128)} %param.23) | copy-start | bytes 1540
  79.2 21.0 %all-to-all-start.3 = ((bf16[16,8,768]{2,1,0:T(8,128)(2,1)}), bf16[16,8,768]{2,1,0:T(8,128)(2,1)S(1)}, u32[]{:S(2)}, u32[]{:S(2)}) async-start(bf16[16,8,768]{2,1,0:T(8,128)(2,1)} %shard_map.138), calls=%async_computation.3 | async-start | bytes 393216 | tf_op jit(solution)/shard_map/all_to_all | solution.py:249
  102.2 23.1 %all-to-all-start.4 = ((bf16[8,144,384]{2,1,0:T(8,128)(2,1)}), bf16[8,144,384]{2,1,0:T(8,128)(2,1)S(1)}, u32[]{:S(2)}, u32[]{:S(2)}) async-start(bf16[8,144,384]{2,1,0:T(8,128)(2,1)} %shard_map.139), calls=%async_computation.4 | async-start | bytes 1769472 | tf_op jit(solution)/shard_map/all_to_all | solution.py:249
  153.7 20.9 %copy-start.3 = (bf16[1,6144,128]{2,1,0:T(8,128)(2,1)S(1)}, bf16[1,6144,128]{2,1,0:T(8,128)(2,1)}, u32[]{:S(2)}) copy-start(bf16[1,6144,128]{2,1,0:T(8,128)(2,1)} %param.25) | copy-start | bytes 4718596
  153.7 20.9 %copy-start.4 = (bf16[1,6144,128]{2,1,0:T(8,128)(2,1)S(1)}, bf16[1,6144,128]{2,1,0:T(8,128)(2,1)}, u32[]{:S(2)}) copy-start(bf16[1,6144,128]{2,1,0:T(8,128)(2,1)} %param.26) | copy-start | bytes 4718596
  174.5 1.3 copy-start.1
  201.3 21.8 %all-to-all-start.6 = ((bf16[4,16,160,128]{3,2,1,0:T(8,128)(2,1)}), bf16[4,16,160,128]{3,2,1,0:T(8,128)(2,1)S(1)}, u32[]{:S(2)}, u32[]{:S(2)}) async-start(bf16[4,16,160,128]{3,2,1,0:T(8,128)(2,1)} %broadcast_in_dim.11), calls=%async_computation.6 | async-start | bytes 5242880 | tf_op jit(solution)/shard_map/all_to_all | solution.py:249
  223.1 1.4 copy-start.2
  226.0 24.5 %all-to-all-start.7 = ((f32[8,20,96]{2,1,0:T(8,128)}), f32[8,20,96]{2,1,0:T(8,128)S(1)}, u32[]{:S(2)}, u32[]{:S(2)}) async-start(f32[8,20,96]{2,1,0:T(8,128)} %reshape.36), calls=%async_computation.7 | async-start | bytes 196608 | tf_op jit(solution)/shard_map/all_to_all | solution.py:249

commit v2 on v1

v2 whole, which is shorter than its diff:
```python
import jax
import jax.numpy as jnp
from jax import lax
from jax.experimental import pallas as pl
from jax.experimental.pallas import tpu as pltpu
from jax.sharding import Mesh, PartitionSpec as P

D = 6144
HD = 128
BLK = 128
CAP = 20
NY, NZ, NE = 4, 16, 8
GROUP = 6
NSEL = 8
FEAT = 96
WIDE = NY * FEAT
TOKB = 128
ROWS = 2 * CAP
FIRST = -1e4
EPS = 1e-05
STATS = 128
R_W = FEAT
R_K = R_W + GROUP * FEAT
R_V = R_K + 4 * BLK
R_ALL = R_V + 4 * BLK
L_ROUTER, L_SQ, L_GAIN = 64, 72, 72
BF, F32 = jnp.bfloat16, jnp.float32
NT = (((1,), (1,)), ((), ()))


def call(body, out_shape, specs, scratch=(), prefetch=0, mib=40):
    params = pltpu.CompilerParams(vmem_limit_bytes=mib * 1024 * 1024)
    outs = jax.tree.map(lambda _: pl.BlockSpec(memory_space=pltpu.VMEM), out_shape)
    grid = pltpu.PrefetchScalarGridSpec(
        num_scalar_prefetch=prefetch,
        grid=(1,),
        in_specs=specs,
        out_specs=outs,
        scratch_shapes=list(scratch),
    )
    return pl.pallas_call(body, out_shape=out_shape, grid_spec=grid, compiler_params=params)


VM = pl.BlockSpec(memory_space=pltpu.VMEM)


def part(*block, at=None):
    at = (0,) * len(block) if at is None else at
    return pl.BlockSpec(block, lambda i, *s: at)


def lanes(rows, width=128):
    return lax.broadcasted_iota(jnp.int32, (rows, width), 1)


def pack_body(k_ref, v_ref, w_ref, x_ref, r_ref, g_ref, o_ref):
    gain = g_ref[...]
    hi = gain.astype(BF).astype(F32)
    mid = (gain - hi).astype(BF).astype(F32)
    lo = gain - hi - mid
    sub = lax.broadcasted_iota(jnp.int32, (8, FEAT), 0)
    gains = jnp.where(sub == 0, hi, jnp.where(sub == 1, mid, jnp.where(sub == 2, lo, 0.0)))
    blank = jnp.zeros((48, FEAT), F32)
    rows = jnp.concatenate([x_ref[...].astype(F32), r_ref[...].astype(F32), gains, blank], axis=0)
    eye = lax.broadcasted_iota(jnp.int32, (FEAT, FEAT), 0) == lanes(FEAT, FEAT)
    misc = lax.dot_general(
        jnp.where(eye, 1.0, 0.0).astype(BF), rows.astype(BF), NT, preferred_element_type=F32
    ).astype(BF)
    for y in range(NY):
        o_ref[y, 0:FEAT, :] = misc
        for g in range(GROUP):
            o_ref[y, R_W + g * FEAT : R_W + (g + 1) * FEAT, :] = w_ref[:, g * 128 : (g + 1) * 128]
        o_ref[y, R_K : R_K + 512, :] = k_ref[...]
        o_ref[y, R_V : R_V + 512, :] = v_ref[...]


def stacked(ref, start):
    return jnp.concatenate([ref[n, start : start + FEAT, :] for n in range(NY)], axis=0)


def attend_body(s_ref, kv_ref, q_ref, o_ref, acc_ref, m_ref, l_ref):
    acc_ref[...] = jnp.zeros_like(acc_ref)
    l_ref[...] = jnp.zeros_like(l_ref)
    m_ref[...] = jnp.full(m_ref.shape, FIRST, F32)
    here = s_ref[NSEL]
    for i in range(NSEL):
        block = s_ref[i]
        owner = block >> 2

        @pl.when((owner & (NZ - 1)) == here)
        def _():
            row = owner >> 4
            start = pl.multiple_of((block & 3) * BLK, BLK)
            keys = kv_ref[row, pl.ds(R_K + start, BLK), :]
            values = kv_ref[row, pl.ds(R_V + start, BLK), :]
            query = jnp.concatenate(
                [q_ref[:, g * HD : (g + 1) * HD] for g in range(GROUP)], axis=0
            )
            s = lax.dot_general(query, keys, NT, preferred_element_type=F32) * HD ** (-0.5)
            old = m_ref[...]
            new = jnp.maximum(old, jnp.max(s, axis=1, keepdims=True))
            p = jnp.exp(s - new).astype(BF)
            keep = jnp.exp(old - new)
            l_ref[...] = l_ref[...] * keep + jnp.sum(p.astype(F32), axis=1, keepdims=True)
            acc_ref[...] = acc_ref[...] * keep + jnp.dot(p, values, preferred_element_type=F32)
            m_ref[...] = new

    lane = lanes(TOKB)
    stats = jnp.zeros((TOKB, 128), F32)
    for g in range(GROUP):
        rows = slice(g * TOKB, (g + 1) * TOKB)
        m, l = m_ref[rows, :], l_ref[rows, :]
        o_ref[:, g * HD : (g + 1) * HD] = (acc_ref[rows, :] / jnp.where(l > 0, l, 1.0)).astype(BF)
        near = m.astype(BF).astype(F32)
        total = l * jnp.exp(m - near)
        high = total.astype(BF).astype(F32)
        stats = jnp.where(lane == g, near, stats)
        stats = jnp.where(lane == 8 + g, high, stats)
        stats = jnp.where(lane == 16 + g, total - high, stats)
    o_ref[:, GROUP * HD :] = stats.astype(BF)


def merge_body(r_ref, o_ref):
    got = r_ref[...].astype(F32)
    stats = got[:, :, GROUP * HD :]
    for g in range(GROUP):
        m = stats[:, :, g : g + 1]
        l = stats[:, :, 8 + g : 9 + g] + stats[:, :, 16 + g : 17 + g]
        weight = l * jnp.exp(m - jnp.max(m, axis=0, keepdims=True))
        top = jnp.sum(weight * got[:, :, g * HD : (g + 1) * HD], axis=0)
        out = (top / jnp.sum(weight, axis=0)).astype(BF)
        o_ref[:, :, g * HD : (g + 1) * HD] = jnp.broadcast_to(out[None], (NZ,) + out.shape)


def project_body(s_ref, a_ref, w_ref, ids_ref, o_ref):
    y, e = s_ref[0], s_ref[1]
    total = jnp.zeros((TOKB, WIDE), F32)
    for g in range(GROUP):
        total += lax.dot_general(
            a_ref[:, g * 128 : (g + 1) * 128],
            stacked(w_ref, R_W + g * FEAT),
            NT,
            preferred_element_type=F32,
        )
    row = lax.broadcasted_iota(jnp.int32, (TOKB, 128), 0)
    mine = (row == lanes(TOKB) + (e & 1) * 64) & (lanes(TOKB) < 64) & ((e >> 1) == y)
    total += lax.dot_general(
        jnp.where(mine, 1.0, 0.0).astype(BF),
        stacked(w_ref, 0),
        NT,
        preferred_element_type=F32,
    )
    out = total.astype(BF)
    for n in range(NE):
        o_ref[n, 0:TOKB, :] = out
        o_ref[n, TOKB:, :] = ids_ref[...]


def pick_body(s_ref, r_ref, w_ref, x_ref, res_ref, side_ref):
    y, e = s_ref[0], s_ref[1]
    total = r_ref[0, 0:TOKB, :].astype(F32)
    for n in range(1, NE):
        total += r_ref[n, 0:TOKB, :].astype(F32)
    ids = r_ref[2 * y, TOKB:, :].astype(F32) + r_ref[2 * y + 1, TOKB:, :].astype(F32)
    id0, id1 = ids[0:1, 0:128], ids[0:1, 128:256]
    base = jnp.where(lanes(1) >= 64, float(CAP), 0.0)
    want = lax.broadcasted_iota(jnp.int32, (ROWS, 128), 0).astype(F32)
    me = e.astype(F32)
    m0 = jnp.where((id0 == me) & (ids[1:2, 0:128] + base == want), 1.0, 0.0)
    m1 = jnp.where((id1 == me) & (ids[1:2, 128:256] + base == want), 1.0, 0.0)
    choose = (m0 + m1).astype(BF)
    other = jnp.sum(m0 * id1 + m1 * id0, axis=1, keepdims=True)
    first = jnp.sum(m0, axis=1, keepdims=True)
    total_high = total.astype(BF)
    total_low = (total - total_high.astype(F32)).astype(BF)
    res = jnp.dot(choose, total_high, preferred_element_type=F32) + jnp.dot(
        choose, total_low, preferred_element_type=F32
    )
    misc = stacked(w_ref, 0)
    sub = lax.broadcasted_iota(jnp.int32, (8, 128), 0)
    take = (lanes(8) == L_GAIN + sub) & (sub < 3)
    gain = lax.dot_general(
        jnp.where(take, 1.0, 0.0).astype(BF), misc, NT, preferred_element_type=F32
    )
    scaled = res * jnp.sum(gain, axis=0, keepdims=True)
    sq = jnp.sum(res * res, axis=1, keepdims=True)
    high = scaled.astype(BF)
    low = (scaled - high.astype(F32)).astype(BF)
    logits = jnp.dot(high, misc, preferred_element_type=F32) + jnp.dot(
        low, misc, preferred_element_type=F32
    )
    lane = lanes(ROWS)
    stats = jnp.where((lane >= L_ROUTER) & (lane < L_ROUTER + 8), logits, 0.0)
    stats = jnp.where(lane == L_SQ, sq, stats)
    stats_high = stats.astype(BF).astype(F32)
    x_ref[:, 0:WIDE] = high
    x_ref[:, WIDE:] = (stats_high + pltpu.roll(stats - stats_high, 64, 1)).astype(BF)
    side_ref[...] = jnp.broadcast_to(other, (ROWS, 128))
    kept = jnp.where(first > 0.5, res, 0.0)
    for n in range(NY):
        for i in range(2):
            rows = slice(i * CAP, (i + 1) * CAP)
            res_ref[n, i] = kept[rows, n * FEAT : (n + 1) * FEAT]


def norm_body(s_ref, g_ref, side_ref, o_ref):
    e = s_ref[1]
    stats = g_ref[0, :, WIDE:].astype(F32)
    for z in range(1, NZ):
        stats += g_ref[z, :, WIDE:].astype(F32)
    stats = stats + pltpu.roll(stats, 64, 1)
    inverse = lax.rsqrt(stats[:, L_SQ : L_SQ + 1] / D + EPS)
    lane = lanes(ROWS)
    mine = jnp.sum(jnp.where(lane == L_ROUTER + e, stats, 0.0), axis=1, keepdims=True)
    rival = jnp.where(lane.astype(F32) == side_ref[...] + float(L_ROUTER), stats, 0.0)
    rival = jnp.sum(rival, axis=1, keepdims=True)
    gate = 1.0 / (1.0 + jnp.exp((rival - mine) * inverse))
    gate_high = gate.astype(BF).astype(F32)
    gates = jnp.where(lane == 0, gate_high, jnp.where(lane == 1, gate - gate_high, 0.0))
    gates = gates.astype(BF)
    for z in range(NZ):
        normed = (g_ref[z, :, 0:WIDE].astype(F32) * inverse).astype(BF)
        for n in range(NY):
            o_ref[n, :, z * WIDE : (z + 1) * WIDE] = normed
    for n in range(NY):
        o_ref[n, :, D:] = gates


def lift_body(x_ref, wg_ref, wu_ref, o_ref):
    gate = jnp.zeros((NY * ROWS, 128), F32)
    lift = jnp.zeros((NY * ROWS, 128), F32)
    for z in range(NZ):
        x = x_ref[:, z * WIDE : (z + 1) * WIDE]
        wg = jnp.concatenate([wg_ref[n, z] for n in range(NY)], axis=0)
        wu = jnp.concatenate([wu_ref[n, z] for n in range(NY)], axis=0)
        gate += jnp.dot(x, wg, preferred_element_type=F32)
        lift += jnp.dot(x, wu, preferred_element_type=F32)
    o_ref[...] = (gate / (1.0 + jnp.exp(-gate)) * lift).astype(BF)


def down_body(s_ref, h_ref, w_ref, gates_ref, res_ref, o_ref):
    y = s_ref[0]
    gates = gates_ref[...].astype(F32)
    gate = gates[:, 0:1] + gates[:, 1:2]
    for n in range(NY):
        total = jnp.zeros((NY * ROWS, FEAT), F32)
        for z in range(0, NZ, 4):
            h = jnp.concatenate([h_ref[z + i] for i in range(4)], axis=1)
            w = w_ref[n, :, z * 128 : (z + 4) * 128]
            total += lax.dot_general(h, w, NT, preferred_element_type=F32)
        total = gate * total
        for i in range(NE):
            o_ref[n, i] = total[i * CAP : (i + 1) * CAP, :]
        for i in range(2):
            o_ref[n, 2 * y + i] += res_ref[n, i]


def swap(x, axis):
    return lax.all_to_all(x, axis, split_axis=0, concat_axis=0, tiled=True)


def shape(*dims, dtype=BF):
    return jax.ShapeDtypeStruct(dims, dtype)


def per_device(
    x_resid,
    queries,
    keys,
    values,
    pattern,
    global_blocks,
    out_weight,
    norm_gain,
    router,
    expert_ids,
    expert_slots,
    w_gate,
    w_up,
    w_down,
):
    y, z, e = lax.axis_index("y"), lax.axis_index("z"), lax.axis_index("exp")
    place = jnp.stack([y, e]).astype(jnp.int32)
    listed = jnp.concatenate([pattern[y], global_blocks, z[None].astype(jnp.int32)])

    pairs = jnp.concatenate([expert_ids.T, expert_slots.T], axis=0).astype(BF)
    blank = jnp.zeros_like(pairs)
    pairs = jnp.where(
        (e & 1) == 0,
        jnp.concatenate([pairs, blank], axis=1),
        jnp.concatenate([blank, pairs], axis=1),
    )
    id_rows = jnp.pad(pairs.reshape(2, 256), ((0, 14), (0, 128)))

    inputs = (keys, values, out_weight.T, x_resid, router.T, norm_gain[None])
    packed = call(
        pack_body, shape(NY, R_ALL, 128), [part(*a.shape) for a in inputs], mib=56
    )(*inputs)
    column = swap(packed, "y")
    block_queries = lax.all_gather(queries, "z", axis=0, tiled=True)

    partial = call(
        attend_body,
        shape(TOKB, (GROUP + 1) * HD),
        [VM] * 2,
        scratch=[pltpu.VMEM((GROUP * TOKB, 128), F32)] * 3,
        prefetch=1,
    )(listed, column, block_queries)
    partial, down = lax.optimization_barrier((partial, w_down[0].T))
    down = down.reshape(FEAT, NY, NZ * 128).swapaxes(0, 1)
    partial = swap(partial.reshape(NZ, TOKB // NZ, (GROUP + 1) * HD), "z")
    attention = call(merge_body, shape(NZ, TOKB // NZ, GROUP * HD), [VM])(partial)
    attention = swap(attention, "z").reshape(TOKB, GROUP * HD)
    products = call(
        project_body,
        shape(NE, TOKB + 16, WIDE),
        [VM, part(NY, R_K, 128), VM],
        prefetch=1,
    )(place, attention, column, id_rows)
    products = swap(products, "exp")
    rows, residual, side = call(
        pick_body,
        (
            shape(ROWS, WIDE + STATS),
            shape(NY, 2, CAP, FEAT, dtype=F32),
            shape(ROWS, 128, dtype=F32),
        ),
        [VM, part(NY, FEAT, 128)],
        prefetch=1,
    )(place, products, column)
    rows, down = lax.optimization_barrier((rows, down))
    down_column = swap(down, "y")
    gathered = lax.all_gather(rows, "z", axis=0)
    gathered, down_column = lax.optimization_barrier((gathered, down_column))
    normed = call(norm_body, shape(NY, ROWS, D + 128), [VM, VM], prefetch=1)(
        place, gathered, side
    )
    normed = swap(normed, "y").reshape(NY * ROWS, D + 128)

    hidden = call(lift_body, shape(NY * ROWS, 128), [VM] * 3)(
        normed, w_gate.reshape(NY, NZ, FEAT, 128), w_up.reshape(NY, NZ, FEAT, 128)
    )
    hidden = lax.all_gather(hidden, "z", axis=0)
    out = call(
        down_body,
        shape(NY, NE, CAP, FEAT, dtype=F32),
        [
            VM,
            VM,
            part(NY * ROWS, 128, at=(0, D // 128)),
            VM,
        ],
        prefetch=1,
    )(place, hidden, down_column, normed, residual)
    back = swap(out.reshape(NY * NE, CAP, FEAT), ("y", "exp")).reshape(NY * NE * CAP, FEAT)
    flat = expert_ids * CAP + expert_slots
    at = jnp.arange(NY * NE * CAP, dtype=jnp.int32)[None, :] % (NE * CAP)
    both = (flat[:, :1] == at).astype(F32) + (flat[:, 1:] == at).astype(F32)
    return jnp.dot(both, back, precision=lax.Precision.HIGHEST).astype(BF)


def solution(mesh):
    inner = Mesh(mesh.devices.reshape(NY, NZ, NE), ("y", "z", "exp"))
    ctx = ("y", "z")
    in_specs = (
        P("exp", ctx),
        P(ctx, "exp"),
        P(ctx, "exp"),
        P(ctx, "exp"),
        P(),
        P(),
        P("exp", ctx),
        P(ctx),
        P(ctx, None),
        P("exp", None),
        P("exp", None),
        P("exp", None, ctx),
        P("exp", None, ctx),
        P("exp", None, ctx),
    )
    return jax.shard_map(
        per_device, mesh=inner, in_specs=in_specs, out_specs=P("exp", ctx), check_vma=False
    )
```

time: 252 us -> 219 us (0.87)
  waiting for transfers between devices: 70.5 us -> 33 us
  blocking collectives: 96.7 us -> 122 us
  starting transfers between devices: 61.5 us -> 47 us
  local copies, waits for them, and re-layouts: 11.7 us -> 2.86 us
    all_to_all x6 -> x5, waiting for transfers between devices: 70.5 us -> 33 us  [swap(): return lax.all_to_all(x, axis, split_axis=0, concat_axis=0, tiled=True)]
    all_gather x0 -> x1, blocking collectives: none -> 30.7 us  [per_device(): block_queries = lax.all_gather(queries, 'z', axis=0, tiled=True)]
    all_to_all x6 -> x5, starting transfers between devices: 61.5 us -> 47 us  [swap(): return lax.all_to_all(x, axis, split_axis=0, concat_axis=0, tiled=True)]
    unnamed x24 -> x14, local copies, waits for them, and re-layouts: 5.9 us -> 0.03 us
    all_to_all x2, blocking collectives: 47 us -> 41.5 us  [swap(): return lax.all_to_all(x, axis, split_axis=0, concat_axis=0, tiled=True)]
    broadcast_in_dim x3 -> x0, local copies, waits for them, and re-layouts: 4.07 us -> none  [the longest x1 1.9 us: per_device(): hidden = swap(jnp.broadcast_to(hidden[None], (NY,) + hidden.shape), 'y')]
  transfers between devices with their start and end apart: 6 -> 5, of which waited for: 6 -> 3; matrix products, arithmetic and copies ran while one was open for 1% -> 1% of each run, Pallas kernels for 1% -> 0%
where the time goes in v2:
time: 219 us; the launch traced here: 218 us
  blocking collectives  122 us (56%)
  starting transfers between devices  47 us (21%)
  waiting for transfers between devices  33 us (15%)
  Pallas kernels  11.9 us (5%)
  local copies, waits for them, and re-layouts  2.86 us (1%)
    all_to_all x5, starting transfers between devices, swap(): return lax.all_to_all(x, axis, split_axis=0, concat_axis=0, tiled=True)  47 us
    all_to_all x2, blocking collectives, swap(): return lax.all_to_all(x, axis, split_axis=0, concat_axis=0, tiled=True)  41.5 us
    all_to_all x5, waiting for transfers between devices, swap(): return lax.all_to_all(x, axis, split_axis=0, concat_axis=0, tiled=True)  33 us
    all_gather x1, blocking collectives, per_device(): block_queries = lax.all_gather(queries, 'z', axis=0, tiled=True)  30.7 us
    all_gather x1, blocking collectives, per_device(): gathered = lax.all_gather(rows, 'z', axis=0)  26.9 us
    all_gather x1, blocking collectives, per_device(): hidden = lax.all_gather(hidden, 'z', axis=0)  23.1 us
  transfers between devices with their start and end apart: 5, of which 3 were waited for; matrix products, arithmetic and copies ran while one was open for 1% of the time, Pallas kernels for 0%

profile of v2, /device:TPU:1, one launch (start us, length us, event | category | flops | bytes accessed | tf_op | source)
XLA Modules:
  0.0 218.4 jit_solution(2201267251245219288)
XLA Ops:
  0.0 0.0 copy-start
  0.0 2.5 %shard_map.136 = bf16[4,1696,128]{2,1,0:T(8,128)(2,1)} custom-call(bf16[512,128]{1,0:T(8,128)(2,1)} %k_ref.1, bf16[512,128]{1,0:T(8,128)(2,1)} %v_ref.1, bf16[96,768]{1,0:T(8,128)(2,1)} %bitcast.45, bf16[64,96]{1,0:T(8,128)(2,1)} %x_ref.1, bf16[8,96]{1,0:T(8,128)(2,1)} %bitcast.46, f32[1,96]{1,0:T(1,128)} %bitcast.47), custom_call_target="tpu_custom_call" | custom-call | tf_op jit(solution)/shard_map/pallas_call | solution.py:296
  2.5 0.0 copy-start.3
  2.5 0.0 copy-start.6
  2.5 5.1 %all-to-all-start = ((bf16[4,1696,128]{2,1,0:T(8,128)(2,1)}), bf16[4,1696,128]{2,1,0:T(8,128)(2,1)S(1)}, u32[]{:S(2)}, u32[]{:S(2)}) async-start(bf16[4,1696,128]{2,1,0:T(8,128)(2,1)} %shard_map.136), calls=%async_computation | async-start | bytes 3473408 | tf_op jit(solution)/shard_map/all_to_all | solution.py:259
  7.7 0.0 copy-done.3
  7.7 30.7 %all_gather.15.q_ref = bf16[128,768]{1,0:T(8,128)(2,1)S(1)} all-gather(bf16[8,768]{1,0:T(8,128)(2,1)S(1)} %copy-done.3), channel_id=1, replica_groups=mesh['y'=4,'z'=16,'exp'=8] {'z'}, dimensions={0}, use_global_device_ids=true | all-gather | bytes 208896 | tf_op jit(solution)/shard_map/all_gather | solution.py:300
  38.4 0.0 copy-done
  38.4 0.0 copy-done.6
  38.4 0.1 pad_add_fusion.1.s_ref
  38.5 0.0 copy-start.4
  38.5 0.0 copy-start.5
  38.5 0.0 all-to-all-done.kv_ref.w_ref
  38.5 0.9 shard_map.137
  39.4 19.7 %all_to_all.35.r_ref = bf16[16,8,896]{2,1,0:T(8,128)(2,1)S(1)} all-to-all(bf16[16,8,896]{2,1,0:T(8,128)(2,1)S(1)} %bitcast.41), channel_id=1, replica_groups=mesh['y'=4,'z'=16,'exp'=8] {'z'}, dimensions={0} | all-to-all | bytes 458752 | tf_op jit(solution)/shard_map/all_to_all | solution.py:259
  59.1 1.2 shard_map.138
  60.3 5.4 %all-to-all-start.2 = ((bf16[16,8,768]{2,1,0:T(8,128)(2,1)}), bf16[16,8,768]{2,1,0:T(8,128)(2,1)S(1)}, u32[]{:S(2)}, u32[]{:S(2)}) async-start(bf16[16,8,768]{2,1,0:T(8,128)(2,1)} %shard_map.138), calls=%async_computation.2 | async-start | bytes 393216 | tf_op jit(solution)/shard_map/all_to_all | solution.py:259
  65.7 0.0 copy-done.4
  65.7 0.0 copy-done.5
  65.8 0.1 pad_select_fusion
  65.9 0.1 pad_add_fusion.s_ref
  66.0 12.2 %all-to-all-done.2 = bf16[16,8,768]{2,1,0:T(8,128)(2,1)S(1)} async-done(((bf16[16,8,768]{2,1,0:T(8,128)(2,1)}), bf16[16,8,768]{2,1,0:T(8,128)(2,1)S(1)}, u32[]{:S(2)}, u32[]{:S(2)}) %all-to-all-start.2) | async-done | bytes 196640 | tf_op jit(solution)/shard_map/all_to_all | solution.py:259
  78.1 1.9 shard_map.139
  80.1 12.8 %all-to-all-start.3 = ((bf16[8,144,384]{2,1,0:T(8,128)(2,1)}), bf16[8,144,384]{2,1,0:T(8,128)(2,1)S(1)}, u32[]{:S(2)}, u32[]{:S(2)}) async-start(bf16[8,144,384]{2,1,0:T(8,128)(2,1)} %shard_map.139), calls=%async_computation.3 | async-start | bytes 1769472 | tf_op jit(solution)/shard_map/all_to_all | solution.py:259
  92.9 2.8 %copy.18 = bf16[12,4,8,2048]{3,2,0,1:T(8,128)(2,1)} copy(bf16[12,4,8,2048]{3,2,1,0:T(8,128)(2,1)} %bitcast.44) | data formatting | bytes 3145728 | tf_op jit(solution)/shard_map/reshape | solution.py:310
  95.7 10.6 %all-to-all-done.3.r_ref = bf16[8,144,384]{2,1,0:T(8,128)(2,1)S(1)} async-done(((bf16[8,144,384]{2,1,0:T(8,128)(2,1)}), bf16[8,144,384]{2,1,0:T(8,128)(2,1)S(1)}, u32[]{:S(2)}, u32[]{:S(2)}) %all-to-all-start.3) | async-done | bytes 884768 | tf_op jit(solution)/shard_map/all_to_all | solution.py:259
  106.3 1.1 shard_map.140
  107.4 4.4 %all-to-all-start.4 = ((bf16[4,96,2048]{2,1,0:T(8,128)(2,1)}), bf16[4,96,2048]{2,1,0:T(8,128)(2,1)S(1)}, u32[]{:S(2)}, u32[]{:S(2)}) async-start(bf16[4,96,2048]{2,1,0:T(8,128)(2,1)} %bitcast.43), calls=%async_computation.4 | async-start | bytes 3145728 | tf_op jit(solution)/shard_map/all_to_all | solution.py:259
  111.7 26.9 %all-gather = bf16[640,512]{1,0:T(8,128)(2,1)S(1)} all-gather(bf16[40,512]{1,0:T(8,128)(2,1)S(1)} %get-tuple-element.17), channel_id=2, replica_groups=mesh['y'=4,'z'=16,'exp'=8] {'z'}, dimensions={0}, use_global_device_ids=true | all-gather | bytes 696320 | tf_op jit(solution)/shard_map/all_gather | solution.py:333
  138.6 0.0 all-to-all-done.4.w_ref
  138.6 0.9 shard_map.141
  139.6 0.0 copy-start.1
  139.6 0.0 copy-start.2
  139.6 21.8 %all_to_all.36 = bf16[4,40,6272]{2,1,0:T(8,128)(2,1)S(1)} all-to-all(bf16[4,40,6272]{2,1,0:T(8,128)(2,1)S(1)} %shard_map.141), channel_id=1, replica_groups=mesh['y'=4,'z'=16,'exp'=8] {'y'}, dimensions={0} | all-to-all | bytes 4014080 | tf_op jit(solution)/shard_map/all_to_all | solution.py:259
  161.4 0.0 copy-done.1
  161.4 0.0 copy-done.2
  161.4 1.2 shard_map.142
  162.6 23.1 %all-gather.1 = bf16[2560,128]{1,0:T(8,128)(2,1)S(1)} all-gather(bf16[160,128]{1,0:T(8,128)(2,1)S(1)} %shard_map.142), channel_id=3, replica_groups=mesh['y'=4,'z'=16,'exp'=8] {'z'}, dimensions={0}, use_global_device_ids=true | all-gather | bytes 696320 | tf_op jit(solution)/shard_map/all_gather | solution.py:343
  185.7 2.1 shard_map.143
  187.9 19.2 %all-to-all-start.6 = ((f32[32,20,96]{2,1,0:T(8,128)}), f32[32,20,96]{2,1,0:T(8,128)S(1)}, u32[]{:S(2)}, u32[]{:S(2)}) async-start(f32[32,20,96]{2,1,0:T(8,128)} %bitcast.21), calls=%async_computation.6 | async-start | bytes 786432 | tf_op jit(solution)/shard_map/all_to_all | solution.py:259
  207.1 10.3 %all-to-all-done.6 = f32[32,20,96]{2,1,0:T(8,128)S(1)} async-done(((f32[32,20,96]{2,1,0:T(8,128)}), f32[32,20,96]{2,1,0:T(8,128)S(1)}, u32[]{:S(2)}, u32[]{:S(2)}) %all-to-all-start.6) | async-done | bytes 245792 | tf_op jit(solution)/shard_map/all_to_all | solution.py:259
  217.4 1.0 convolution_convert_fusion
  (8 shorter events, 0.1 us)
Async XLA Ops:
  0.0 38.4 %copy-start = (s32[4,6]{1,0:T(4,128)S(1)}, s32[4,6]{1,0:T(4,128)}, u32[]{:S(2)}) copy-start(s32[4,6]{1,0:T(4,128)} %param.18) | copy-start | bytes 292
  2.5 5.2 %copy-start.3 = (bf16[8,768]{1,0:T(8,128)(2,1)S(1)}, bf16[8,768]{1,0:T(8,128)(2,1)}, u32[]{:S(2)}) copy-start(bf16[8,768]{1,0:T(8,128)(2,1)} %param.15) | copy-start | bytes 36868
  2.5 35.8 %copy-start.6 = (s32[2]{0:T(128)S(1)}, s32[2]{0:T(128)}, u32[]{:S(2)}) copy-start(s32[2]{0:T(128)} %param.19) | copy-start | bytes 28
  2.5 35.9 %all-to-all-start = ((bf16[4,1696,128]{2,1,0:T(8,128)(2,1)}), bf16[4,1696,128]{2,1,0:T(8,128)(2,1)S(1)}, u32[]{:S(2)}, u32[]{:S(2)}) async-start(bf16[4,1696,128]{2,1,0:T(8,128)(2,1)} %shard_map.136), calls=%async_computation | async-start | bytes 3473408 | tf_op jit(solution)/shard_map/all_to_all | solution.py:259
  38.5 27.3 %copy-start.4 = (s32[64,2]{0,1:T(2,128)S(1)}, s32[64,2]{0,1:T(2,128)}, u32[]{:S(2)}) copy-start(s32[64,2]{0,1:T(2,128)} %param.24) | copy-start | bytes 1540
  38.5 27.3 %copy-start.5 = (s32[64,2]{0,1:T(2,128)S(1)}, s32[64,2]{0,1:T(2,128)}, u32[]{:S(2)}) copy-start(s32[64,2]{0,1:T(2,128)} %param.23) | copy-start | bytes 1540
  60.3 17.9 %all-to-all-start.2 = ((bf16[16,8,768]{2,1,0:T(8,128)(2,1)}), bf16[16,8,768]{2,1,0:T(8,128)(2,1)S(1)}, u32[]{:S(2)}, u32[]{:S(2)}) async-start(bf16[16,8,768]{2,1,0:T(8,128)(2,1)} %shard_map.138), calls=%async_computation.2 | async-start | bytes 393216 | tf_op jit(solution)/shard_map/all_to_all | solution.py:259
  80.1 26.2 %all-to-all-start.3 = ((bf16[8,144,384]{2,1,0:T(8,128)(2,1)}), bf16[8,144,384]{2,1,0:T(8,128)(2,1)S(1)}, u32[]{:S(2)}, u32[]{:S(2)}) async-start(bf16[8,144,384]{2,1,0:T(8,128)(2,1)} %shard_map.139), calls=%async_computation.3 | async-start | bytes 1769472 | tf_op jit(solution)/shard_map/all_to_all | solution.py:259
  107.4 31.2 %all-to-all-start.4 = ((bf16[4,96,2048]{2,1,0:T(8,128)(2,1)}), bf16[4,96,2048]{2,1,0:T(8,128)(2,1)S(1)}, u32[]{:S(2)}, u32[]{:S(2)}) async-start(bf16[4,96,2048]{2,1,0:T(8,128)(2,1)} %bitcast.43), calls=%async_computation.4 | async-start | bytes 3145728 | tf_op jit(solution)/shard_map/all_to_all | solution.py:259
  139.6 21.8 %copy-start.1 = (bf16[1,6144,128]{2,1,0:T(8,128)(2,1)S(1)}, bf16[1,6144,128]{2,1,0:T(8,128)(2,1)}, u32[]{:S(2)}) copy-start(bf16[1,6144,128]{2,1,0:T(8,128)(2,1)} %param.25) | copy-start | bytes 4718596
  139.6 21.8 %copy-start.2 = (bf16[1,6144,128]{2,1,0:T(8,128)(2,1)S(1)}, bf16[1,6144,128]{2,1,0:T(8,128)(2,1)}, u32[]{:S(2)}) copy-start(bf16[1,6144,128]{2,1,0:T(8,128)(2,1)} %param.26) | copy-start | bytes 4718596
  187.9 29.5 %all-to-all-start.6 = ((f32[32,20,96]{2,1,0:T(8,128)}), f32[32,20,96]{2,1,0:T(8,128)S(1)}, u32[]{:S(2)}, u32[]{:S(2)}) async-start(f32[32,20,96]{2,1,0:T(8,128)} %bitcast.21), calls=%async_computation.6 | async-start | bytes 786432 | tf_op jit(solution)/shard_map/all_to_all | solution.py:259

commit v3 on v2

--- a/solution.py
+++ b/solution.py
@@ -132,6 +132,13 @@
         o_ref[:, :, g * HD : (g + 1) * HD] = jnp.broadcast_to(out[None], (NZ,) + out.shape)
 
 
+def slot_keys(ids_ref):
+    ids = ids_ref[0].astype(F32) + ids_ref[1].astype(F32)
+    id0, id1, slot0, slot1 = (ids[i : i + 1, :] for i in range(4))
+    base = jnp.where(lanes(1) >= 64, float(CAP), 0.0)
+    return id0 * ROWS + slot0 + base, id1 * ROWS + slot1 + base, id0, id1
+
+
 def project_body(s_ref, a_ref, w_ref, ids_ref, o_ref):
     y, e = s_ref[0], s_ref[1]
     total = jnp.zeros((TOKB, WIDE), F32)
@@ -150,32 +157,23 @@
         NT,
         preferred_element_type=F32,
     )
-    out = total.astype(BF)
-    for n in range(NE):
-        o_ref[n, 0:TOKB, :] = out
-        o_ref[n, TOKB:, :] = ids_ref[...]
-
-
-def pick_body(s_ref, r_ref, w_ref, x_ref, res_ref, side_ref):
-    y, e = s_ref[0], s_ref[1]
-    total = r_ref[0, 0:TOKB, :].astype(F32)
+    key0, key1, _, _ = slot_keys(ids_ref)
+    want = lax.broadcasted_iota(jnp.int32, (NE * ROWS, 128), 0).astype(F32)
+    choose = jnp.where((key0 == want) | (key1 == want), 1.0, 0.0).astype(BF)
+    o_ref[...] = jnp.dot(choose, total.astype(BF), preferred_element_type=F32).astype(BF)
+
+
+def pick_body(s_ref, r_ref, w_ref, ids_ref, x_ref, res_ref, side_ref):
+    e = s_ref[1]
+    res = r_ref[0].astype(F32)
     for n in range(1, NE):
-        total += r_ref[n, 0:TOKB, :].astype(F32)
-    ids = r_ref[2 * y, TOKB:, :].astype(F32) + r_ref[2 * y + 1, TOKB:, :].astype(F32)
-    id0, id1 = ids[0:1, 0:128], ids[0:1, 128:256]
-    base = jnp.where(lanes(1) >= 64, float(CAP), 0.0)
-    want = lax.broadcasted_iota(jnp.int32, (ROWS, 128), 0).astype(F32)
-    me = e.astype(F32)
-    m0 = jnp.where((id0 == me) & (ids[1:2, 0:128] + base == want), 1.0, 0.0)
-    m1 = jnp.where((id1 == me) & (ids[1:2, 128:256] + base == want), 1.0, 0.0)
-    choose = (m0 + m1).astype(BF)
+        res += r_ref[n].astype(F32)
+    key0, key1, id0, id1 = slot_keys(ids_ref)
+    want = (lax.broadcasted_iota(jnp.int32, (ROWS, 128), 0) + e * ROWS).astype(F32)
+    m0 = jnp.where(key0 == want, 1.0, 0.0)
+    m1 = jnp.where(key1 == want, 1.0, 0.0)
     other = jnp.sum(m0 * id1 + m1 * id0, axis=1, keepdims=True)
     first = jnp.sum(m0, axis=1, keepdims=True)
-    total_high = total.astype(BF)
-    total_low = (total - total_high.astype(F32)).astype(BF)
-    res = jnp.dot(choose, total_high, preferred_element_type=F32) + jnp.dot(
-        choose, total_low, preferred_element_type=F32
-    )
     misc = stacked(w_ref, 0)
     sub = lax.broadcasted_iota(jnp.int32, (8, 128), 0)
     take = (lanes(8) == L_GAIN + sub) & (sub < 3)
@@ -196,11 +194,7 @@
     x_ref[:, 0:WIDE] = high
     x_ref[:, WIDE:] = (stats_high + pltpu.roll(stats - stats_high, 64, 1)).astype(BF)
     side_ref[...] = jnp.broadcast_to(other, (ROWS, 128))
-    kept = jnp.where(first > 0.5, res, 0.0)
-    for n in range(NY):
-        for i in range(2):
-            rows = slice(i * CAP, (i + 1) * CAP)
-            res_ref[n, i] = kept[rows, n * FEAT : (n + 1) * FEAT]
+    res_ref[...] = jnp.where(first > 0.5, res, 0.0)
 
 
 def norm_body(s_ref, g_ref, side_ref, o_ref):
@@ -238,21 +232,25 @@
     o_ref[...] = (gate / (1.0 + jnp.exp(-gate)) * lift).astype(BF)
 
 
-def down_body(s_ref, h_ref, w_ref, gates_ref, res_ref, o_ref):
+def down_body(s_ref, h_ref, w_ref, gates_ref, res_ref, o_ref, sum_ref):
     y = s_ref[0]
     gates = gates_ref[...].astype(F32)
     gate = gates[:, 0:1] + gates[:, 1:2]
+    mine = pl.ds(pl.multiple_of(y * ROWS, 8), ROWS)
+    sums = jnp.zeros((NY * ROWS, WIDE), F32)
+    for z in range(0, NZ, 4):
+        h = jnp.concatenate([h_ref[z + i] for i in range(4)], axis=1)
+        w = jnp.concatenate(
+            [w_ref[n, :, z * 128 : (z + 4) * 128] for n in range(NY)], axis=0
+        )
+        sums += lax.dot_general(h, w, NT, preferred_element_type=F32)
+    sum_ref[...] = gate * sums
+    sum_ref[mine, :] += res_ref[...]
+    total = sum_ref[...]
     for n in range(NY):
-        total = jnp.zeros((NY * ROWS, FEAT), F32)
-        for z in range(0, NZ, 4):
-            h = jnp.concatenate([h_ref[z + i] for i in range(4)], axis=1)
-            w = w_ref[n, :, z * 128 : (z + 4) * 128]
-            total += lax.dot_general(h, w, NT, preferred_element_type=F32)
-        total = gate * total
         for i in range(NE):
-            o_ref[n, i] = total[i * CAP : (i + 1) * CAP, :]
-        for i in range(2):
-            o_ref[n, 2 * y + i] += res_ref[n, i]
+            piece = total[i * CAP : (i + 1) * CAP, n * FEAT : (n + 1) * FEAT]
+            o_ref[n, i] = piece.astype(BF)
 
 
 def swap(x, axis):
@@ -290,7 +288,7 @@
         jnp.concatenate([pairs, blank], axis=1),
         jnp.concatenate([blank, pairs], axis=1),
     )
-    id_rows = jnp.pad(pairs.reshape(2, 256), ((0, 14), (0, 128)))
+    pairs = jnp.pad(pairs, ((0, 12), (0, 0)))
 
     inputs = (keys, values, out_weight.T, x_resid, router.T, norm_gain[None])
     packed = call(
@@ -311,23 +309,33 @@
     partial = swap(partial.reshape(NZ, TOKB // NZ, (GROUP + 1) * HD), "z")
     attention = call(merge_body, shape(NZ, TOKB // NZ, GROUP * HD), [VM])(partial)
     attention = swap(attention, "z").reshape(TOKB, GROUP * HD)
+    ids = []
+    for flip in range(2):
+        route = [
+            ((to_e >> 1) * NE + 2 * to_y + ((to_e & 1) ^ flip), to_y * NE + to_e)
+            for to_y in range(NY)
+            for to_e in range(NE)
+        ]
+        ids.append(lax.ppermute(pairs, ("y", "exp"), route))
+    attention, *ids = lax.optimization_barrier((attention, *ids))
+    ids = jnp.stack(ids)
     products = call(
         project_body,
-        shape(NE, TOKB + 16, WIDE),
-        [VM, part(NY, R_K, 128), VM],
+        shape(NE * ROWS, WIDE),
+        [VM, VM, VM],
         prefetch=1,
-    )(place, attention, column, id_rows)
-    products = swap(products, "exp")
+    )(place, attention, column, ids)
+    products = swap(products.reshape(NE, ROWS, WIDE), "exp")
     rows, residual, side = call(
         pick_body,
         (
             shape(ROWS, WIDE + STATS),
-            shape(NY, 2, CAP, FEAT, dtype=F32),
+            shape(ROWS, WIDE, dtype=F32),
             shape(ROWS, 128, dtype=F32),
         ),
-        [VM, part(NY, FEAT, 128)],
+        [VM, VM, VM],
         prefetch=1,
-    )(place, products, column)
+    )(place, products, column, ids)
     rows, down = lax.optimization_barrier((rows, down))
     down_column = swap(down, "y")
     gathered = lax.all_gather(rows, "z", axis=0)
@@ -343,20 +351,21 @@
     hidden = lax.all_gather(hidden, "z", axis=0)
     out = call(
         down_body,
-        shape(NY, NE, CAP, FEAT, dtype=F32),
+        shape(NY, NE, CAP, FEAT),
         [
             VM,
             VM,
             part(NY * ROWS, 128, at=(0, D // 128)),
             VM,
         ],
+        scratch=[pltpu.VMEM((NY * ROWS, WIDE), F32)],
         prefetch=1,
     )(place, hidden, down_column, normed, residual)
     back = swap(out.reshape(NY * NE, CAP, FEAT), ("y", "exp")).reshape(NY * NE * CAP, FEAT)
     flat = expert_ids * CAP + expert_slots
     at = jnp.arange(NY * NE * CAP, dtype=jnp.int32)[None, :] % (NE * CAP)
-    both = (flat[:, :1] == at).astype(F32) + (flat[:, 1:] == at).astype(F32)
-    return jnp.dot(both, back, precision=lax.Precision.HIGHEST).astype(BF)
+    both = ((flat[:, :1] == at) | (flat[:, 1:] == at)).astype(BF)
+    return jnp.dot(both, back, preferred_element_type=F32).astype(BF)
 
 
 def solution(mesh):

time: 219 us -> 212 us (0.968)
  waiting for transfers between devices: 33 us -> 14.3 us
  starting transfers between devices: 47 us -> 56.7 us
    all_to_all x5, waiting for transfers between devices: 33 us -> 13.5 us  [swap(): return lax.all_to_all(x, axis, split_axis=0, concat_axis=0, tiled=True)]
    ppermute x0 -> x2, starting transfers between devices: none -> 9.87 us  [per_device(): ids.append(lax.ppermute(pairs, ('y', 'exp'), route))]
  transfers between devices with their start and end apart: 5 -> 7, of which waited for: 3 -> 4; matrix products, arithmetic and copies ran while one was open for 1% -> 1% of each run, Pallas kernels for 0% -> 0%
where the time goes in v3:
time: 212 us; the launch traced here: 211 us
  blocking collectives  124 us (58%)
  starting transfers between devices  56.7 us (27%)
  waiting for transfers between devices  14.3 us (7%)
  Pallas kernels  12 us (6%)
  local copies, waits for them, and re-layouts  2.86 us (1%)
    all_to_all x5, starting transfers between devices, swap(): return lax.all_to_all(x, axis, split_axis=0, concat_axis=0, tiled=True)  46.8 us
    all_to_all x2, blocking collectives, swap(): return lax.all_to_all(x, axis, split_axis=0, concat_axis=0, tiled=True)  40.7 us
    all_gather x1, blocking collectives, per_device(): block_queries = lax.all_gather(queries, 'z', axis=0, tiled=True)  30.7 us
    all_gather x1, blocking collectives, per_device(): gathered = lax.all_gather(rows, 'z', axis=0)  27.7 us
    all_gather x1, blocking collectives, per_device(): hidden = lax.all_gather(hidden, 'z', axis=0)  24.9 us
    all_to_all x5, waiting for transfers between devices, swap(): return lax.all_to_all(x, axis, split_axis=0, concat_axis=0, tiled=True)  13.5 us
    ppermute x2, starting transfers between devices, per_device(): ids.append(lax.ppermute(pairs, ('y', 'exp'), route))  9.87 us
  transfers between devices with their start and end apart: 7, of which 4 were waited for; matrix products, arithmetic and copies ran while one was open for 1% of the time, Pallas kernels for 0%

profile of v3, /device:TPU:1, one launch (start us, length us, event | category | flops | bytes accessed | tf_op | source)
XLA Modules:
  0.0 211.0 jit_solution(4328416930984462392)
XLA Ops:
  0.0 0.0 copy-start
  0.0 2.5 %shard_map.136 = bf16[4,1696,128]{2,1,0:T(8,128)(2,1)} custom-call(bf16[512,128]{1,0:T(8,128)(2,1)} %k_ref.1, bf16[512,128]{1,0:T(8,128)(2,1)} %v_ref.1, bf16[96,768]{1,0:T(8,128)(2,1)} %bitcast.48, bf16[64,96]{1,0:T(8,128)(2,1)} %x_ref.1, bf16[8,96]{1,0:T(8,128)(2,1)} %bitcast.51, f32[1,96]{1,0:T(1,128)} %bitcast.52), custom_call_target="tpu_custom_call" | custom-call | tf_op jit(solution)/shard_map/pallas_call | solution.py:294
  2.5 0.0 copy-start.3
  2.5 0.0 copy-start.6
  2.5 5.1 %all-to-all-start = ((bf16[4,1696,128]{2,1,0:T(8,128)(2,1)}), bf16[4,1696,128]{2,1,0:T(8,128)(2,1)S(1)}, u32[]{:S(2)}, u32[]{:S(2)}) async-start(bf16[4,1696,128]{2,1,0:T(8,128)(2,1)} %shard_map.136), calls=%async_computation | async-start | bytes 3473408 | tf_op jit(solution)/shard_map/all_to_all | solution.py:257
  7.7 0.0 copy-done.3
  7.7 30.7 %all_gather.15.q_ref = bf16[128,768]{1,0:T(8,128)(2,1)S(1)} all-gather(bf16[8,768]{1,0:T(8,128)(2,1)S(1)} %copy-done.3), channel_id=1, replica_groups=mesh['y'=4,'z'=16,'exp'=8] {'z'}, dimensions={0}, use_global_device_ids=true | all-gather | bytes 208896 | tf_op jit(solution)/shard_map/all_gather | solution.py:298
  38.4 0.0 copy-done
  38.4 0.0 copy-done.6
  38.4 0.1 pad_add_fusion.1.s_ref
  38.5 0.0 copy-start.4
  38.5 0.0 copy-start.5
  38.5 0.0 all-to-all-done.kv_ref.w_ref
  38.5 1.4 shard_map.137
  39.8 19.3 %all_to_all.35.r_ref = bf16[16,8,896]{2,1,0:T(8,128)(2,1)S(1)} all-to-all(bf16[16,8,896]{2,1,0:T(8,128)(2,1)S(1)} %bitcast.44), channel_id=1, replica_groups=mesh['y'=4,'z'=16,'exp'=8] {'z'}, dimensions={0} | all-to-all | bytes 458752 | tf_op jit(solution)/shard_map/all_to_all | solution.py:257
  59.1 1.2 shard_map.138
  60.3 5.4 %all-to-all-start.2 = ((bf16[16,8,768]{2,1,0:T(8,128)(2,1)}), bf16[16,8,768]{2,1,0:T(8,128)(2,1)S(1)}, u32[]{:S(2)}, u32[]{:S(2)}) async-start(bf16[16,8,768]{2,1,0:T(8,128)(2,1)} %shard_map.138), calls=%async_computation.2 | async-start | bytes 393216 | tf_op jit(solution)/shard_map/all_to_all | solution.py:257
  65.7 0.0 copy-done.4
  65.7 0.0 copy-done.5
  65.8 0.1 pad_select_fusion
  65.9 0.7 collective-permute-start
  66.5 9.2 %collective-permute-start.1 = (bf16[16,128]{1,0:T(8,128)(2,1)S(1)}, bf16[16,128]{1,0:T(8,128)(2,1)S(1)}, u32[]{:S(2)}, u32[]{:S(2)}) collective-permute-start(bf16[16,128]{1,0:T(8,128)(2,1)S(1)} %pad.6), channel_id=1, source_target_pairs={{1,0},{0,1},{129,2},{128,3},{257,4},{256,5},{385,6},{384,7},{3,128... | collective-permute-start | bytes 12296 | tf_op jit(solution)/shard_map/ppermute | solution.py:319
  75.8 0.1 pad_add_fusion.s_ref
  75.8 0.0 collective-permute-done
  75.8 0.7 collective-permute-done.1
  76.6 1.6 all-to-all-done.2
  78.2 1.9 shard_map.139
  80.0 14.0 %all-to-all-start.3 = ((bf16[8,40,384]{2,1,0:T(8,128)(2,1)}), bf16[8,40,384]{2,1,0:T(8,128)(2,1)S(1)}, u32[]{:S(2)}, u32[]{:S(2)}) async-start(bf16[8,40,384]{2,1,0:T(8,128)(2,1)} %bitcast.17), calls=%async_computation.3 | async-start | bytes 491520 | tf_op jit(solution)/shard_map/all_to_all | solution.py:257
  94.1 2.8 %copy.18 = bf16[12,4,8,2048]{3,2,0,1:T(8,128)(2,1)} copy(bf16[12,4,8,2048]{3,2,1,0:T(8,128)(2,1)} %bitcast.47) | data formatting | bytes 3145728 | tf_op jit(solution)/shard_map/reshape | solution.py:308
  96.8 3.6 %all-to-all-done.3.r_ref = bf16[8,40,384]{2,1,0:T(8,128)(2,1)S(1)} async-done(((bf16[8,40,384]{2,1,0:T(8,128)(2,1)}), bf16[8,40,384]{2,1,0:T(8,128)(2,1)S(1)}, u32[]{:S(2)}, u32[]{:S(2)}) %all-to-all-start.3) | async-done | bytes 245792 | tf_op jit(solution)/shard_map/all_to_all | solution.py:257
  100.4 0.9 shard_map.140
  101.3 3.7 %all-to-all-start.4 = ((bf16[4,96,2048]{2,1,0:T(8,128)(2,1)}), bf16[4,96,2048]{2,1,0:T(8,128)(2,1)S(1)}, u32[]{:S(2)}, u32[]{:S(2)}) async-start(bf16[4,96,2048]{2,1,0:T(8,128)(2,1)} %bitcast.46), calls=%async_computation.4 | async-start | bytes 3145728 | tf_op jit(solution)/shard_map/all_to_all | solution.py:257
  105.0 27.7 %all-gather = bf16[640,512]{1,0:T(8,128)(2,1)S(1)} all-gather(bf16[40,512]{1,0:T(8,128)(2,1)S(1)} %get-tuple-element.23), channel_id=2, replica_groups=mesh['y'=4,'z'=16,'exp'=8] {'z'}, dimensions={0}, use_global_device_ids=true | all-gather | bytes 696320 | tf_op jit(solution)/shard_map/all_gather | solution.py:341
  132.7 0.0 all-to-all-done.4.w_ref
  132.7 0.9 shard_map.141
  133.6 0.0 copy-start.1
  133.6 0.0 copy-start.2
  133.6 21.4 %all_to_all.36 = bf16[4,40,6272]{2,1,0:T(8,128)(2,1)S(1)} all-to-all(bf16[4,40,6272]{2,1,0:T(8,128)(2,1)S(1)} %shard_map.141), channel_id=1, replica_groups=mesh['y'=4,'z'=16,'exp'=8] {'y'}, dimensions={0} | all-to-all | bytes 4014080 | tf_op jit(solution)/shard_map/all_to_all | solution.py:257
  155.0 0.0 copy-done.1
  155.0 0.0 copy-done.2
  155.0 1.2 shard_map.142
  156.3 24.9 %all-gather.1 = bf16[2560,128]{1,0:T(8,128)(2,1)S(1)} all-gather(bf16[160,128]{1,0:T(8,128)(2,1)S(1)} %shard_map.142), channel_id=3, replica_groups=mesh['y'=4,'z'=16,'exp'=8] {'z'}, dimensions={0}, use_global_device_ids=true | all-gather | bytes 696320 | tf_op jit(solution)/shard_map/all_gather | solution.py:351
  181.2 2.0 shard_map.143
  183.2 18.5 %all-to-all-start.6 = ((bf16[32,20,96]{2,1,0:T(8,128)(2,1)}), bf16[32,20,96]{2,1,0:T(8,128)(2,1)S(1)}, u32[]{:S(2)}, u32[]{:S(2)}) async-start(bf16[32,20,96]{2,1,0:T(8,128)(2,1)} %bitcast.24), calls=%async_computation.6 | async-start | bytes 393216 | tf_op jit(solution)/shard_map/all_to_all | solution.py:257
  201.8 8.3 %all-to-all-done.6 = bf16[32,20,96]{2,1,0:T(8,128)(2,1)S(1)} async-done(((bf16[32,20,96]{2,1,0:T(8,128)(2,1)}), bf16[32,20,96]{2,1,0:T(8,128)(2,1)S(1)}, u32[]{:S(2)}, u32[]{:S(2)}) %all-to-all-start.6) | async-done | bytes 122912 | tf_op jit(solution)/shard_map/all_to_all | solution.py:257
  210.1 0.1 reshape.50
  210.2 0.8 convolution_convert_fusion
  (7 shorter events, 0.0 us)
Async XLA Ops:
  0.0 38.4 %copy-start = (s32[4,6]{1,0:T(4,128)S(1)}, s32[4,6]{1,0:T(4,128)}, u32[]{:S(2)}) copy-start(s32[4,6]{1,0:T(4,128)} %param.18) | copy-start | bytes 292
  2.5 5.2 %copy-start.3 = (bf16[8,768]{1,0:T(8,128)(2,1)S(1)}, bf16[8,768]{1,0:T(8,128)(2,1)}, u32[]{:S(2)}) copy-start(bf16[8,768]{1,0:T(8,128)(2,1)} %param.15) | copy-start | bytes 36868
  2.5 35.8 %copy-start.6 = (s32[2]{0:T(128)S(1)}, s32[2]{0:T(128)}, u32[]{:S(2)}) copy-start(s32[2]{0:T(128)} %param.19) | copy-start | bytes 28
  2.5 35.9 %all-to-all-start = ((bf16[4,1696,128]{2,1,0:T(8,128)(2,1)}), bf16[4,1696,128]{2,1,0:T(8,128)(2,1)S(1)}, u32[]{:S(2)}, u32[]{:S(2)}) async-start(bf16[4,1696,128]{2,1,0:T(8,128)(2,1)} %shard_map.136), calls=%async_computation | async-start | bytes 3473408 | tf_op jit(solution)/shard_map/all_to_all | solution.py:257
  38.5 27.3 %copy-start.4 = (s32[64,2]{0,1:T(2,128)S(1)}, s32[64,2]{0,1:T(2,128)}, u32[]{:S(2)}) copy-start(s32[64,2]{0,1:T(2,128)} %param.24) | copy-start | bytes 1540
  38.5 27.3 %copy-start.5 = (s32[64,2]{0,1:T(2,128)S(1)}, s32[64,2]{0,1:T(2,128)}, u32[]{:S(2)}) copy-start(s32[64,2]{0,1:T(2,128)} %param.23) | copy-start | bytes 1540
  60.3 17.9 %all-to-all-start.2 = ((bf16[16,8,768]{2,1,0:T(8,128)(2,1)}), bf16[16,8,768]{2,1,0:T(8,128)(2,1)S(1)}, u32[]{:S(2)}, u32[]{:S(2)}) async-start(bf16[16,8,768]{2,1,0:T(8,128)(2,1)} %shard_map.138), calls=%async_computation.2 | async-start | bytes 393216 | tf_op jit(solution)/shard_map/all_to_all | solution.py:257
  65.9 10.0 %collective-permute-start = (bf16[16,128]{1,0:T(8,128)(2,1)S(1)}, bf16[16,128]{1,0:T(8,128)(2,1)S(1)}, u32[]{:S(2)}, u32[]{:S(2)}) collective-permute-start(bf16[16,128]{1,0:T(8,128)(2,1)S(1)} %pad.6), channel_id=1, source_target_pairs={{0,0},{1,1},{128,2},{129,3},{256,4},{257,5},{384,6},{385,7},{2,128... | collective-permute-start | bytes 12296 | tf_op jit(solution)/shard_map/ppermute | solution.py:319
  66.5 10.0 %collective-permute-start.1 = (bf16[16,128]{1,0:T(8,128)(2,1)S(1)}, bf16[16,128]{1,0:T(8,128)(2,1)S(1)}, u32[]{:S(2)}, u32[]{:S(2)}) collective-permute-start(bf16[16,128]{1,0:T(8,128)(2,1)S(1)} %pad.6), channel_id=1, source_target_pairs={{1,0},{0,1},{129,2},{128,3},{257,4},{256,5},{385,6},{384,7},{3,128... | collective-permute-start | bytes 12296 | tf_op jit(solution)/shard_map/ppermute | solution.py:319
  80.0 20.4 %all-to-all-start.3 = ((bf16[8,40,384]{2,1,0:T(8,128)(2,1)}), bf16[8,40,384]{2,1,0:T(8,128)(2,1)S(1)}, u32[]{:S(2)}, u32[]{:S(2)}) async-start(bf16[8,40,384]{2,1,0:T(8,128)(2,1)} %bitcast.17), calls=%async_computation.3 | async-start | bytes 491520 | tf_op jit(solution)/shard_map/all_to_all | solution.py:257
  101.3 31.3 %all-to-all-start.4 = ((bf16[4,96,2048]{2,1,0:T(8,128)(2,1)}), bf16[4,96,2048]{2,1,0:T(8,128)(2,1)S(1)}, u32[]{:S(2)}, u32[]{:S(2)}) async-start(bf16[4,96,2048]{2,1,0:T(8,128)(2,1)} %bitcast.46), calls=%async_computation.4 | async-start | bytes 3145728 | tf_op jit(solution)/shard_map/all_to_all | solution.py:257
  133.6 21.4 %copy-start.1 = (bf16[1,6144,128]{2,1,0:T(8,128)(2,1)S(1)}, bf16[1,6144,128]{2,1,0:T(8,128)(2,1)}, u32[]{:S(2)}) copy-start(bf16[1,6144,128]{2,1,0:T(8,128)(2,1)} %param.25) | copy-start | bytes 4718596
  133.6 21.4 %copy-start.2 = (bf16[1,6144,128]{2,1,0:T(8,128)(2,1)S(1)}, bf16[1,6144,128]{2,1,0:T(8,128)(2,1)}, u32[]{:S(2)}) copy-start(bf16[1,6144,128]{2,1,0:T(8,128)(2,1)} %param.26) | copy-start | bytes 4718596
  183.2 26.9 %all-to-all-start.6 = ((bf16[32,20,96]{2,1,0:T(8,128)(2,1)}), bf16[32,20,96]{2,1,0:T(8,128)(2,1)S(1)}, u32[]{:S(2)}, u32[]{:S(2)}) async-start(bf16[32,20,96]{2,1,0:T(8,128)(2,1)} %bitcast.24), calls=%async_computation.6 | async-start | bytes 393216 | tf_op jit(solution)/shard_map/all_to_all | solution.py:257

commit v4 on v3

--- a/solution.py
+++ b/solution.py
@@ -133,7 +133,7 @@
 
 
 def slot_keys(ids_ref):
-    ids = ids_ref[0].astype(F32) + ids_ref[1].astype(F32)
+    ids = ids_ref[...].astype(F32)
     id0, id1, slot0, slot1 = (ids[i : i + 1, :] for i in range(4))
     base = jnp.where(lanes(1) >= 64, float(CAP), 0.0)
     return id0 * ROWS + slot0 + base, id1 * ROWS + slot1 + base, id0, id1
@@ -306,19 +306,19 @@
     )(listed, column, block_queries)
     partial, down = lax.optimization_barrier((partial, w_down[0].T))
     down = down.reshape(FEAT, NY, NZ * 128).swapaxes(0, 1)
+    twins = pairs + lax.ppermute(pairs, "exp", [(i, i ^ 1) for i in range(NE)])
     partial = swap(partial.reshape(NZ, TOKB // NZ, (GROUP + 1) * HD), "z")
+    partial, twins = lax.optimization_barrier((partial, twins))
     attention = call(merge_body, shape(NZ, TOKB // NZ, GROUP * HD), [VM])(partial)
     attention = swap(attention, "z").reshape(TOKB, GROUP * HD)
-    ids = []
-    for flip in range(2):
-        route = [
-            ((to_e >> 1) * NE + 2 * to_y + ((to_e & 1) ^ flip), to_y * NE + to_e)
-            for to_y in range(NY)
-            for to_e in range(NE)
-        ]
-        ids.append(lax.ppermute(pairs, ("y", "exp"), route))
-    attention, *ids = lax.optimization_barrier((attention, *ids))
-    ids = jnp.stack(ids)
+    route = [
+        ((to_e >> 1) * NE + 2 * to_y + (to_e & 1), to_y * NE + to_e)
+        for to_y in range(NY)
+        for to_e in range(NE)
+    ]
+    ids = lax.ppermute(twins, ("y", "exp"), route)
+    attention, ids = lax.optimization_barrier((attention, ids))
+
     products = call(
         project_body,
         shape(NE * ROWS, WIDE),

time: 212 us -> 209 us (0.986)
  blocking collectives: 124 us -> 101 us
  waiting for transfers between devices: 14.3 us -> 27.9 us
  starting transfers between devices: 56.7 us -> 63.4 us
    all_to_all x2 -> x1, blocking collectives: 40.7 us -> 21.2 us  [swap(): return lax.all_to_all(x, axis, split_axis=0, concat_axis=0, tiled=True)]
    all_to_all x5 -> x6, waiting for transfers between devices: 13.5 us -> 27.1 us  [swap(): return lax.all_to_all(x, axis, split_axis=0, concat_axis=0, tiled=True)]
    all_to_all x5 -> x6, starting transfers between devices: 46.8 us -> 54.6 us  [swap(): return lax.all_to_all(x, axis, split_axis=0, concat_axis=0, tiled=True)]
  transfers between devices with their start and end apart: 7 -> 8, of which waited for: 4 -> 5; matrix products, arithmetic and copies ran while one was open for 1% -> 1% of each run, Pallas kernels for 0% -> 0%
where the time goes in v4:
time: 209 us
  blocking collectives  101 us (48%)
  starting transfers between devices  63.4 us (30%)
  waiting for transfers between devices  27.9 us (13%)
  Pallas kernels  12.3 us (6%)
  local copies, waits for them, and re-layouts  2.86 us (1%)
    all_to_all x6, starting transfers between devices, swap(): return lax.all_to_all(x, axis, split_axis=0, concat_axis=0, tiled=True)  54.6 us
    all_gather x1, blocking collectives, per_device(): block_queries = lax.all_gather(queries, 'z', axis=0, tiled=True)  30.8 us
    all_to_all x6, waiting for transfers between devices, swap(): return lax.all_to_all(x, axis, split_axis=0, concat_axis=0, tiled=True)  27.1 us
    all_gather x1, blocking collectives, per_device(): gathered = lax.all_gather(rows, 'z', axis=0)  25.8 us
    all_gather x1, blocking collectives, per_device(): hidden = lax.all_gather(hidden, 'z', axis=0)  23.2 us
    all_to_all x1, blocking collectives, swap(): return lax.all_to_all(x, axis, split_axis=0, concat_axis=0, tiled=True)  21.2 us
    ppermute x1, starting transfers between devices, per_device(): twins = pairs + lax.ppermute(pairs, 'exp', [(i, i ^ 1) for i in range(NE)])  8.22 us
  transfers between devices with their start and end apart: 8, of which 5 were waited for; matrix products, arithmetic and copies ran while one was open for 1% of the time, Pallas kernels for 0%

profile of v4, /device:TPU:1, one launch (start us, length us, event | category | flops | bytes accessed | tf_op | source)
XLA Modules:
  0.0 208.7 jit_solution(10975970949647859429)
XLA Ops:
  0.0 0.0 copy-start
  0.0 2.5 %shard_map.136 = bf16[4,1696,128]{2,1,0:T(8,128)(2,1)} custom-call(bf16[512,128]{1,0:T(8,128)(2,1)} %k_ref.1, bf16[512,128]{1,0:T(8,128)(2,1)} %v_ref.1, bf16[96,768]{1,0:T(8,128)(2,1)} %bitcast.45, bf16[64,96]{1,0:T(8,128)(2,1)} %x_ref.1, bf16[8,96]{1,0:T(8,128)(2,1)} %bitcast.46, f32[1,96]{1,0:T(1,128)} %bitcast.47), custom_call_target="tpu_custom_call" | custom-call | tf_op jit(solution)/shard_map/pallas_call | solution.py:294
  2.5 0.0 copy-start.3
  2.5 0.0 copy-start.6
  2.5 5.1 %all-to-all-start = ((bf16[4,1696,128]{2,1,0:T(8,128)(2,1)}), bf16[4,1696,128]{2,1,0:T(8,128)(2,1)S(1)}, u32[]{:S(2)}, u32[]{:S(2)}) async-start(bf16[4,1696,128]{2,1,0:T(8,128)(2,1)} %shard_map.136), calls=%async_computation | async-start | bytes 3473408 | tf_op jit(solution)/shard_map/all_to_all | solution.py:257
  7.7 0.0 copy-start.4
  7.7 0.0 copy-start.5
  7.7 0.0 copy-done.3
  7.7 30.8 %all_gather.15.q_ref = bf16[128,768]{1,0:T(8,128)(2,1)S(1)} all-gather(bf16[8,768]{1,0:T(8,128)(2,1)S(1)} %copy-done.3), channel_id=1, replica_groups=mesh['y'=4,'z'=16,'exp'=8] {'z'}, dimensions={0}, use_global_device_ids=true | all-gather | bytes 208896 | tf_op jit(solution)/shard_map/all_gather | solution.py:298
  38.5 0.0 copy-done
  38.5 0.0 copy-done.6
  38.5 0.1 pad_add_fusion.2.s_ref
  38.6 0.0 all-to-all-done.kv_ref.w_ref
  38.6 1.6 shard_map.137
  40.2 7.1 %all-to-all-start.1 = ((bf16[16,8,896]{2,1,0:T(8,128)(2,1)}), bf16[16,8,896]{2,1,0:T(8,128)(2,1)S(1)}, u32[]{:S(2)}, u32[]{:S(2)}) async-start(bf16[16,8,896]{2,1,0:T(8,128)(2,1)} %bitcast.11), calls=%async_computation.1 | async-start | bytes 458752 | tf_op jit(solution)/shard_map/all_to_all | solution.py:257
  47.3 0.0 copy-done.4
  47.3 0.0 copy-done.5
  47.4 0.1 pad_select_fusion
  47.5 8.2 %collective-permute-start = (bf16[16,128]{1,0:T(8,128)(2,1)S(1)}, bf16[16,128]{1,0:T(8,128)(2,1)S(1)}, u32[]{:S(2)}, u32[]{:S(2)}) collective-permute-start(bf16[16,128]{1,0:T(8,128)(2,1)S(1)} %pad.6), channel_id=1, source_target_pairs={{0,1},{1,0},{2,3},{3,2},{4,5},{5,4},{6,7},{7,6},{8,9},{9,8},{10,11... | collective-permute-start | bytes 12296 | tf_op jit(solution)/shard_map/ppermute | solution.py:309
  55.7 0.8 collective-permute-done
  56.5 3.5 %all-to-all-done.1.r_ref = bf16[16,8,896]{2,1,0:T(8,128)(2,1)S(1)} async-done(((bf16[16,8,896]{2,1,0:T(8,128)(2,1)}), bf16[16,8,896]{2,1,0:T(8,128)(2,1)S(1)}, u32[]{:S(2)}, u32[]{:S(2)}) %all-to-all-start.1) | async-done | bytes 229408 | tf_op jit(solution)/shard_map/all_to_all | solution.py:257
  60.0 1.2 shard_map.138
  61.2 8.2 %all-to-all-start.2 = ((bf16[16,8,768]{2,1,0:T(8,128)(2,1)}), bf16[16,8,768]{2,1,0:T(8,128)(2,1)S(1)}, u32[]{:S(2)}, u32[]{:S(2)}) async-start(bf16[16,8,768]{2,1,0:T(8,128)(2,1)} %shard_map.138), calls=%async_computation.2 | async-start | bytes 393216 | tf_op jit(solution)/shard_map/all_to_all | solution.py:257
  69.4 0.7 collective-permute-start.1
  70.1 0.1 pad_add_fusion.1.s_ref
  70.2 0.0 collective-permute-done.1.ids_ref
  70.2 11.6 %all-to-all-done.2 = bf16[16,8,768]{2,1,0:T(8,128)(2,1)S(1)} async-done(((bf16[16,8,768]{2,1,0:T(8,128)(2,1)}), bf16[16,8,768]{2,1,0:T(8,128)(2,1)S(1)}, u32[]{:S(2)}, u32[]{:S(2)}) %all-to-all-start.2) | async-done | bytes 196640 | tf_op jit(solution)/shard_map/all_to_all | solution.py:257
  81.8 1.9 shard_map.139
  83.6 10.2 %all-to-all-start.3 = ((bf16[8,40,384]{2,1,0:T(8,128)(2,1)}), bf16[8,40,384]{2,1,0:T(8,128)(2,1)S(1)}, u32[]{:S(2)}, u32[]{:S(2)}) async-start(bf16[8,40,384]{2,1,0:T(8,128)(2,1)} %bitcast.15), calls=%async_computation.3 | async-start | bytes 491520 | tf_op jit(solution)/shard_map/all_to_all | solution.py:257
  93.9 2.7 %copy.18 = bf16[12,4,8,2048]{3,2,0,1:T(8,128)(2,1)} copy(bf16[12,4,8,2048]{3,2,1,0:T(8,128)(2,1)} %bitcast.44) | data formatting | bytes 3145728 | tf_op jit(solution)/shard_map/reshape | solution.py:308
  96.6 3.6 %all-to-all-done.3.r_ref = bf16[8,40,384]{2,1,0:T(8,128)(2,1)S(1)} async-done(((bf16[8,40,384]{2,1,0:T(8,128)(2,1)}), bf16[8,40,384]{2,1,0:T(8,128)(2,1)S(1)}, u32[]{:S(2)}, u32[]{:S(2)}) %all-to-all-start.3) | async-done | bytes 245792 | tf_op jit(solution)/shard_map/all_to_all | solution.py:257
  100.2 0.9 shard_map.140
  101.1 4.7 %all-to-all-start.4 = ((bf16[4,96,2048]{2,1,0:T(8,128)(2,1)}), bf16[4,96,2048]{2,1,0:T(8,128)(2,1)S(1)}, u32[]{:S(2)}, u32[]{:S(2)}) async-start(bf16[4,96,2048]{2,1,0:T(8,128)(2,1)} %bitcast.43), calls=%async_computation.4 | async-start | bytes 3145728 | tf_op jit(solution)/shard_map/all_to_all | solution.py:257
  105.8 25.8 %all-gather = bf16[640,512]{1,0:T(8,128)(2,1)S(1)} all-gather(bf16[40,512]{1,0:T(8,128)(2,1)S(1)} %get-tuple-element.25), channel_id=2, replica_groups=mesh['y'=4,'z'=16,'exp'=8] {'z'}, dimensions={0}, use_global_device_ids=true | all-gather | bytes 696320 | tf_op jit(solution)/shard_map/all_gather | solution.py:341
  131.7 0.0 all-to-all-done.4.w_ref
  131.7 0.9 shard_map.141
  132.6 0.0 copy-start.1
  132.6 0.0 copy-start.2
  132.7 21.2 %all_to_all.35 = bf16[4,40,6272]{2,1,0:T(8,128)(2,1)S(1)} all-to-all(bf16[4,40,6272]{2,1,0:T(8,128)(2,1)S(1)} %shard_map.141), channel_id=1, replica_groups=mesh['y'=4,'z'=16,'exp'=8] {'y'}, dimensions={0} | all-to-all | bytes 4014080 | tf_op jit(solution)/shard_map/all_to_all | solution.py:257
  153.8 0.0 copy-done.1
  153.8 0.0 copy-done.2
  153.8 1.2 shard_map.142
  155.1 23.2 %all-gather.1 = bf16[2560,128]{1,0:T(8,128)(2,1)S(1)} all-gather(bf16[160,128]{1,0:T(8,128)(2,1)S(1)} %shard_map.142), channel_id=3, replica_groups=mesh['y'=4,'z'=16,'exp'=8] {'z'}, dimensions={0}, use_global_device_ids=true | all-gather | bytes 696320 | tf_op jit(solution)/shard_map/all_gather | solution.py:351
  178.3 2.0 shard_map.143
  180.3 19.1 %all-to-all-start.6 = ((bf16[32,20,96]{2,1,0:T(8,128)(2,1)}), bf16[32,20,96]{2,1,0:T(8,128)(2,1)S(1)}, u32[]{:S(2)}, u32[]{:S(2)}) async-start(bf16[32,20,96]{2,1,0:T(8,128)(2,1)} %bitcast.22), calls=%async_computation.6 | async-start | bytes 393216 | tf_op jit(solution)/shard_map/all_to_all | solution.py:257
  199.5 8.3 %all-to-all-done.6 = bf16[32,20,96]{2,1,0:T(8,128)(2,1)S(1)} async-done(((bf16[32,20,96]{2,1,0:T(8,128)(2,1)}), bf16[32,20,96]{2,1,0:T(8,128)(2,1)S(1)}, u32[]{:S(2)}, u32[]{:S(2)}) %all-to-all-start.6) | async-done | bytes 122912 | tf_op jit(solution)/shard_map/all_to_all | solution.py:257
  207.8 0.1 reshape.50
  207.9 0.8 convolution_convert_fusion
  (7 shorter events, 0.1 us)
Async XLA Ops:
  0.0 38.5 %copy-start = (s32[4,6]{1,0:T(4,128)S(1)}, s32[4,6]{1,0:T(4,128)}, u32[]{:S(2)}) copy-start(s32[4,6]{1,0:T(4,128)} %param.18) | copy-start | bytes 292
  2.5 5.2 %copy-start.3 = (bf16[8,768]{1,0:T(8,128)(2,1)S(1)}, bf16[8,768]{1,0:T(8,128)(2,1)}, u32[]{:S(2)}) copy-start(bf16[8,768]{1,0:T(8,128)(2,1)} %param.15) | copy-start | bytes 36868
  2.5 36.0 %copy-start.6 = (s32[2]{0:T(128)S(1)}, s32[2]{0:T(128)}, u32[]{:S(2)}) copy-start(s32[2]{0:T(128)} %param.19) | copy-start | bytes 28
  2.5 36.1 %all-to-all-start = ((bf16[4,1696,128]{2,1,0:T(8,128)(2,1)}), bf16[4,1696,128]{2,1,0:T(8,128)(2,1)S(1)}, u32[]{:S(2)}, u32[]{:S(2)}) async-start(bf16[4,1696,128]{2,1,0:T(8,128)(2,1)} %shard_map.136), calls=%async_computation | async-start | bytes 3473408 | tf_op jit(solution)/shard_map/all_to_all | solution.py:257
  7.7 39.7 %copy-start.4 = (s32[64,2]{0,1:T(2,128)S(1)}, s32[64,2]{0,1:T(2,128)}, u32[]{:S(2)}) copy-start(s32[64,2]{0,1:T(2,128)} %param.24) | copy-start | bytes 1540
  7.7 39.7 %copy-start.5 = (s32[64,2]{0,1:T(2,128)S(1)}, s32[64,2]{0,1:T(2,128)}, u32[]{:S(2)}) copy-start(s32[64,2]{0,1:T(2,128)} %param.23) | copy-start | bytes 1540
  40.2 19.8 %all-to-all-start.1 = ((bf16[16,8,896]{2,1,0:T(8,128)(2,1)}), bf16[16,8,896]{2,1,0:T(8,128)(2,1)S(1)}, u32[]{:S(2)}, u32[]{:S(2)}) async-start(bf16[16,8,896]{2,1,0:T(8,128)(2,1)} %bitcast.11), calls=%async_computation.1 | async-start | bytes 458752 | tf_op jit(solution)/shard_map/all_to_all | solution.py:257
  47.5 9.0 %collective-permute-start = (bf16[16,128]{1,0:T(8,128)(2,1)S(1)}, bf16[16,128]{1,0:T(8,128)(2,1)S(1)}, u32[]{:S(2)}, u32[]{:S(2)}) collective-permute-start(bf16[16,128]{1,0:T(8,128)(2,1)S(1)} %pad.6), channel_id=1, source_target_pairs={{0,1},{1,0},{2,3},{3,2},{4,5},{5,4},{6,7},{7,6},{8,9},{9,8},{10,11... | collective-permute-start | bytes 12296 | tf_op jit(solution)/shard_map/ppermute | solution.py:309
  61.2 20.6 %all-to-all-start.2 = ((bf16[16,8,768]{2,1,0:T(8,128)(2,1)}), bf16[16,8,768]{2,1,0:T(8,128)(2,1)S(1)}, u32[]{:S(2)}, u32[]{:S(2)}) async-start(bf16[16,8,768]{2,1,0:T(8,128)(2,1)} %shard_map.138), calls=%async_computation.2 | async-start | bytes 393216 | tf_op jit(solution)/shard_map/all_to_all | solution.py:257
  69.4 0.8 collective-permute-start.1
  83.6 16.6 %all-to-all-start.3 = ((bf16[8,40,384]{2,1,0:T(8,128)(2,1)}), bf16[8,40,384]{2,1,0:T(8,128)(2,1)S(1)}, u32[]{:S(2)}, u32[]{:S(2)}) async-start(bf16[8,40,384]{2,1,0:T(8,128)(2,1)} %bitcast.15), calls=%async_computation.3 | async-start | bytes 491520 | tf_op jit(solution)/shard_map/all_to_all | solution.py:257
  101.1 30.5 %all-to-all-start.4 = ((bf16[4,96,2048]{2,1,0:T(8,128)(2,1)}), bf16[4,96,2048]{2,1,0:T(8,128)(2,1)S(1)}, u32[]{:S(2)}, u32[]{:S(2)}) async-start(bf16[4,96,2048]{2,1,0:T(8,128)(2,1)} %bitcast.43), calls=%async_computation.4 | async-start | bytes 3145728 | tf_op jit(solution)/shard_map/all_to_all | solution.py:257
  132.6 21.2 %copy-start.1 = (bf16[1,6144,128]{2,1,0:T(8,128)(2,1)S(1)}, bf16[1,6144,128]{2,1,0:T(8,128)(2,1)}, u32[]{:S(2)}) copy-start(bf16[1,6144,128]{2,1,0:T(8,128)(2,1)} %param.25) | copy-start | bytes 4718596
  132.6 21.2 %copy-start.2 = (bf16[1,6144,128]{2,1,0:T(8,128)(2,1)S(1)}, bf16[1,6144,128]{2,1,0:T(8,128)(2,1)}, u32[]{:S(2)}) copy-start(bf16[1,6144,128]{2,1,0:T(8,128)(2,1)} %param.26) | copy-start | bytes 4718596
  180.3 27.5 %all-to-all-start.6 = ((bf16[32,20,96]{2,1,0:T(8,128)(2,1)}), bf16[32,20,96]{2,1,0:T(8,128)(2,1)S(1)}, u32[]{:S(2)}, u32[]{:S(2)}) async-start(bf16[32,20,96]{2,1,0:T(8,128)(2,1)} %bitcast.22), calls=%async_computation.6 | async-start | bytes 393216 | tf_op jit(solution)/shard_map/all_to_all | solution.py:257

commit v5 on v4

--- a/solution.py
+++ b/solution.py
@@ -308,7 +308,7 @@
     down = down.reshape(FEAT, NY, NZ * 128).swapaxes(0, 1)
     twins = pairs + lax.ppermute(pairs, "exp", [(i, i ^ 1) for i in range(NE)])
     partial = swap(partial.reshape(NZ, TOKB // NZ, (GROUP + 1) * HD), "z")
-    partial, twins = lax.optimization_barrier((partial, twins))
+    partial, twins, down = lax.optimization_barrier((partial, twins, down))
     attention = call(merge_body, shape(NZ, TOKB // NZ, GROUP * HD), [VM])(partial)
     attention = swap(attention, "z").reshape(TOKB, GROUP * HD)
     route = [

time: 209 us -> 210 us (level)
  blocking collectives: 101 us -> 118 us
  starting transfers between devices: 63.4 us -> 54.8 us
  waiting for transfers between devices: 27.9 us -> 22.9 us
    all_to_all x1 -> x2, blocking collectives: 21.2 us -> 38.5 us  [swap(): return lax.all_to_all(x, axis, split_axis=0, concat_axis=0, tiled=True)]
    all_to_all x6 -> x5, starting transfers between devices: 54.6 us -> 45.9 us  [swap(): return lax.all_to_all(x, axis, split_axis=0, concat_axis=0, tiled=True)]
    all_to_all x6 -> x5, waiting for transfers between devices: 27.1 us -> 22.1 us  [swap(): return lax.all_to_all(x, axis, split_axis=0, concat_axis=0, tiled=True)]
  transfers between devices with their start and end apart: 8 -> 7, of which waited for: 5 -> 4; matrix products, arithmetic and copies ran while one was open for 1% -> 1% of each run, Pallas kernels for 0% -> 0%
where the time goes in v5:
time: 210 us
  blocking collectives  118 us (56%)
  starting transfers between devices  54.8 us (26%)
  waiting for transfers between devices  22.9 us (11%)
  Pallas kernels  11.6 us (6%)
    all_to_all x5, starting transfers between devices, swap(): return lax.all_to_all(x, axis, split_axis=0, concat_axis=0, tiled=True)  45.9 us
    all_to_all x2, blocking collectives, swap(): return lax.all_to_all(x, axis, split_axis=0, concat_axis=0, tiled=True)  38.5 us
    all_gather x1, blocking collectives, per_device(): block_queries = lax.all_gather(queries, 'z', axis=0, tiled=True)  30.8 us
    all_gather x1, blocking collectives, per_device(): gathered = lax.all_gather(rows, 'z', axis=0)  25.7 us
    all_gather x1, blocking collectives, per_device(): hidden = lax.all_gather(hidden, 'z', axis=0)  23.1 us
    all_to_all x5, waiting for transfers between devices, swap(): return lax.all_to_all(x, axis, split_axis=0, concat_axis=0, tiled=True)  22.1 us
    ppermute x1, starting transfers between devices, per_device(): twins = pairs + lax.ppermute(pairs, 'exp', [(i, i ^ 1) for i in range(NE)])  8.24 us
  transfers between devices with their start and end apart: 7, of which 4 were waited for; matrix products, arithmetic and copies ran while one was open for 1% of the time, Pallas kernels for 0%

profile of v5, /device:TPU:1, one launch (start us, length us, event | category | flops | bytes accessed | tf_op | source)
XLA Modules:
  0.0 210.1 jit_solution(9395447997861489548)
XLA Ops:
  0.0 0.0 copy-start
  0.0 2.5 %shard_map.136 = bf16[4,1696,128]{2,1,0:T(8,128)(2,1)} custom-call(bf16[512,128]{1,0:T(8,128)(2,1)} %k_ref.1, bf16[512,128]{1,0:T(8,128)(2,1)} %v_ref.1, bf16[96,768]{1,0:T(8,128)(2,1)} %bitcast.45, bf16[64,96]{1,0:T(8,128)(2,1)} %x_ref.1, bf16[8,96]{1,0:T(8,128)(2,1)} %bitcast.46, f32[1,96]{1,0:T(1,128)} %bitcast.47), custom_call_target="tpu_custom_call" | custom-call | tf_op jit(solution)/shard_map/pallas_call | solution.py:294
  2.5 0.0 copy-start.4
  2.5 0.0 copy-start.7
  2.5 5.1 %all-to-all-start = ((bf16[4,1696,128]{2,1,0:T(8,128)(2,1)}), bf16[4,1696,128]{2,1,0:T(8,128)(2,1)S(1)}, u32[]{:S(2)}, u32[]{:S(2)}) async-start(bf16[4,1696,128]{2,1,0:T(8,128)(2,1)} %shard_map.136), calls=%async_computation | async-start | bytes 3473408 | tf_op jit(solution)/shard_map/all_to_all | solution.py:257
  7.7 0.0 copy-start.5
  7.7 0.0 copy-start.6
  7.7 0.0 copy-done.4
  7.7 30.8 %all_gather.15.q_ref = bf16[128,768]{1,0:T(8,128)(2,1)S(1)} all-gather(bf16[8,768]{1,0:T(8,128)(2,1)S(1)} %copy-done.4), channel_id=1, replica_groups=mesh['y'=4,'z'=16,'exp'=8] {'z'}, dimensions={0}, use_global_device_ids=true | all-gather | bytes 208896 | tf_op jit(solution)/shard_map/all_gather | solution.py:298
  38.5 0.0 copy-done
  38.5 0.0 copy-done.7
  38.6 0.1 pad_add_fusion.2.s_ref
  38.6 0.0 all-to-all-done.kv_ref.w_ref
  38.6 1.6 shard_map.137
  40.2 7.5 %all-to-all-start.1 = ((bf16[16,8,896]{2,1,0:T(8,128)(2,1)}), bf16[16,8,896]{2,1,0:T(8,128)(2,1)S(1)}, u32[]{:S(2)}, u32[]{:S(2)}) async-start(bf16[16,8,896]{2,1,0:T(8,128)(2,1)} %bitcast.11), calls=%async_computation.1 | async-start | bytes 458752 | tf_op jit(solution)/shard_map/all_to_all | solution.py:257
  47.8 0.0 copy-done.5
  47.8 0.0 copy-done.6
  47.8 0.1 pad_select_fusion
  47.9 8.2 %collective-permute-start = (bf16[16,128]{1,0:T(8,128)(2,1)S(1)}, bf16[16,128]{1,0:T(8,128)(2,1)S(1)}, u32[]{:S(2)}, u32[]{:S(2)}) collective-permute-start(bf16[16,128]{1,0:T(8,128)(2,1)S(1)} %pad.6), channel_id=1, source_target_pairs={{0,1},{1,0},{2,3},{3,2},{4,5},{5,4},{6,7},{7,6},{8,9},{9,8},{10,11... | collective-permute-start | bytes 12296 | tf_op jit(solution)/shard_map/ppermute | solution.py:309
  56.2 0.8 collective-permute-done
  57.0 0.0 copy-done.3
  57.0 1.3 copy.18
  58.3 2.2 %all-to-all-done.1.r_ref = bf16[16,8,896]{2,1,0:T(8,128)(2,1)S(1)} async-done(((bf16[16,8,896]{2,1,0:T(8,128)(2,1)}), bf16[16,8,896]{2,1,0:T(8,128)(2,1)S(1)}, u32[]{:S(2)}, u32[]{:S(2)}) %all-to-all-start.1) | async-done | bytes 229408 | tf_op jit(solution)/shard_map/all_to_all | solution.py:257
  60.4 1.2 shard_map.138
  61.6 9.6 %all-to-all-start.2 = ((bf16[16,8,768]{2,1,0:T(8,128)(2,1)}), bf16[16,8,768]{2,1,0:T(8,128)(2,1)S(1)}, u32[]{:S(2)}, u32[]{:S(2)}) async-start(bf16[16,8,768]{2,1,0:T(8,128)(2,1)} %shard_map.138), calls=%async_computation.2 | async-start | bytes 393216 | tf_op jit(solution)/shard_map/all_to_all | solution.py:257
  71.2 0.7 collective-permute-start.1
  71.8 0.1 pad_add_fusion.1.s_ref
  71.9 0.0 collective-permute-done.1.ids_ref
  71.9 11.6 %all-to-all-done.2 = bf16[16,8,768]{2,1,0:T(8,128)(2,1)S(1)} async-done(((bf16[16,8,768]{2,1,0:T(8,128)(2,1)}), bf16[16,8,768]{2,1,0:T(8,128)(2,1)S(1)}, u32[]{:S(2)}, u32[]{:S(2)}) %all-to-all-start.2) | async-done | bytes 196640 | tf_op jit(solution)/shard_map/all_to_all | solution.py:257
  83.5 1.2 shard_map.139
  84.7 16.9 %all_to_all.35.r_ref = bf16[8,40,384]{2,1,0:T(8,128)(2,1)S(1)} all-to-all(bf16[8,40,384]{2,1,0:T(8,128)(2,1)S(1)} %bitcast.42), channel_id=1, replica_groups=mesh['y'=4,'z'=16,'exp'=8] {'exp'}, dimensions={0} | all-to-all | bytes 491520 | tf_op jit(solution)/shard_map/all_to_all | solution.py:257
  101.6 0.9 shard_map.140
  102.5 4.5 %all-to-all-start.4 = ((bf16[4,96,2048]{2,1,0:T(8,128)(2,1)}), bf16[4,96,2048]{2,1,0:T(8,128)(2,1)S(1)}, u32[]{:S(2)}, u32[]{:S(2)}) async-start(bf16[4,96,2048]{2,1,0:T(8,128)(2,1)} %bitcast.35), calls=%async_computation.4 | async-start | bytes 3145728 | tf_op jit(solution)/shard_map/all_to_all | solution.py:257
  107.0 25.7 %all-gather = bf16[640,512]{1,0:T(8,128)(2,1)S(1)} all-gather(bf16[40,512]{1,0:T(8,128)(2,1)S(1)} %get-tuple-element.27), channel_id=2, replica_groups=mesh['y'=4,'z'=16,'exp'=8] {'z'}, dimensions={0}, use_global_device_ids=true | all-gather | bytes 696320 | tf_op jit(solution)/shard_map/all_gather | solution.py:341
  132.7 0.0 all-to-all-done.4.w_ref
  132.7 0.9 shard_map.141
  133.6 0.0 copy-start.1
  133.6 0.0 copy-start.2
  133.7 21.6 %all_to_all.36 = bf16[4,40,6272]{2,1,0:T(8,128)(2,1)S(1)} all-to-all(bf16[4,40,6272]{2,1,0:T(8,128)(2,1)S(1)} %shard_map.141), channel_id=1, replica_groups=mesh['y'=4,'z'=16,'exp'=8] {'y'}, dimensions={0} | all-to-all | bytes 4014080 | tf_op jit(solution)/shard_map/all_to_all | solution.py:257
  155.3 0.0 copy-done.1
  155.3 0.0 copy-done.2
  155.3 1.2 shard_map.142
  156.5 23.1 %all-gather.1 = bf16[2560,128]{1,0:T(8,128)(2,1)S(1)} all-gather(bf16[160,128]{1,0:T(8,128)(2,1)S(1)} %shard_map.142), channel_id=3, replica_groups=mesh['y'=4,'z'=16,'exp'=8] {'z'}, dimensions={0}, use_global_device_ids=true | all-gather | bytes 696320 | tf_op jit(solution)/shard_map/all_gather | solution.py:351
  179.6 2.0 shard_map.143
  181.6 19.2 %all-to-all-start.6 = ((bf16[32,20,96]{2,1,0:T(8,128)(2,1)}), bf16[32,20,96]{2,1,0:T(8,128)(2,1)S(1)}, u32[]{:S(2)}, u32[]{:S(2)}) async-start(bf16[32,20,96]{2,1,0:T(8,128)(2,1)} %bitcast.22), calls=%async_computation.6 | async-start | bytes 393216 | tf_op jit(solution)/shard_map/all_to_all | solution.py:257
  200.8 8.3 %all-to-all-done.6 = bf16[32,20,96]{2,1,0:T(8,128)(2,1)S(1)} async-done(((bf16[32,20,96]{2,1,0:T(8,128)(2,1)}), bf16[32,20,96]{2,1,0:T(8,128)(2,1)S(1)}, u32[]{:S(2)}, u32[]{:S(2)}) %all-to-all-start.6) | async-done | bytes 122912 | tf_op jit(solution)/shard_map/all_to_all | solution.py:257
  209.2 0.1 reshape.50
  209.2 0.8 convolution_convert_fusion
  (8 shorter events, 0.1 us)
Async XLA Ops:
  0.0 38.5 %copy-start = (s32[4,6]{1,0:T(4,128)S(1)}, s32[4,6]{1,0:T(4,128)}, u32[]{:S(2)}) copy-start(s32[4,6]{1,0:T(4,128)} %param.18) | copy-start | bytes 292
  2.5 5.2 %copy-start.4 = (bf16[8,768]{1,0:T(8,128)(2,1)S(1)}, bf16[8,768]{1,0:T(8,128)(2,1)}, u32[]{:S(2)}) copy-start(bf16[8,768]{1,0:T(8,128)(2,1)} %param.15) | copy-start | bytes 36868
  2.5 36.0 %copy-start.7 = (s32[2]{0:T(128)S(1)}, s32[2]{0:T(128)}, u32[]{:S(2)}) copy-start(s32[2]{0:T(128)} %param.19) | copy-start | bytes 28
  2.5 36.1 %all-to-all-start = ((bf16[4,1696,128]{2,1,0:T(8,128)(2,1)}), bf16[4,1696,128]{2,1,0:T(8,128)(2,1)S(1)}, u32[]{:S(2)}, u32[]{:S(2)}) async-start(bf16[4,1696,128]{2,1,0:T(8,128)(2,1)} %shard_map.136), calls=%async_computation | async-start | bytes 3473408 | tf_op jit(solution)/shard_map/all_to_all | solution.py:257
  7.7 40.1 %copy-start.5 = (s32[64,2]{0,1:T(2,128)S(1)}, s32[64,2]{0,1:T(2,128)}, u32[]{:S(2)}) copy-start(s32[64,2]{0,1:T(2,128)} %param.24) | copy-start | bytes 1540
  7.7 40.1 %copy-start.6 = (s32[64,2]{0,1:T(2,128)S(1)}, s32[64,2]{0,1:T(2,128)}, u32[]{:S(2)}) copy-start(s32[64,2]{0,1:T(2,128)} %param.23) | copy-start | bytes 1540
  7.7 49.3 %copy-start.3 = (bf16[1,8192,96]{1,2,0:T(8,128)(2,1)S(1)}, bf16[1,8192,96]{1,2,0:T(8,128)(2,1)}, u32[]{:S(2)}) copy-start(bf16[1,8192,96]{1,2,0:T(8,128)(2,1)} %param.27) | copy-start | bytes 4718596
  40.2 20.2 %all-to-all-start.1 = ((bf16[16,8,896]{2,1,0:T(8,128)(2,1)}), bf16[16,8,896]{2,1,0:T(8,128)(2,1)S(1)}, u32[]{:S(2)}, u32[]{:S(2)}) async-start(bf16[16,8,896]{2,1,0:T(8,128)(2,1)} %bitcast.11), calls=%async_computation.1 | async-start | bytes 458752 | tf_op jit(solution)/shard_map/all_to_all | solution.py:257
  47.9 9.0 %collective-permute-start = (bf16[16,128]{1,0:T(8,128)(2,1)S(1)}, bf16[16,128]{1,0:T(8,128)(2,1)S(1)}, u32[]{:S(2)}, u32[]{:S(2)}) collective-permute-start(bf16[16,128]{1,0:T(8,128)(2,1)S(1)} %pad.6), channel_id=1, source_target_pairs={{0,1},{1,0},{2,3},{3,2},{4,5},{5,4},{6,7},{7,6},{8,9},{9,8},{10,11... | collective-permute-start | bytes 12296 | tf_op jit(solution)/shard_map/ppermute | solution.py:309
  61.6 21.9 %all-to-all-start.2 = ((bf16[16,8,768]{2,1,0:T(8,128)(2,1)}), bf16[16,8,768]{2,1,0:T(8,128)(2,1)S(1)}, u32[]{:S(2)}, u32[]{:S(2)}) async-start(bf16[16,8,768]{2,1,0:T(8,128)(2,1)} %shard_map.138), calls=%async_computation.2 | async-start | bytes 393216 | tf_op jit(solution)/shard_map/all_to_all | solution.py:257
  71.2 0.8 collective-permute-start.1
  102.5 30.2 %all-to-all-start.4 = ((bf16[4,96,2048]{2,1,0:T(8,128)(2,1)}), bf16[4,96,2048]{2,1,0:T(8,128)(2,1)S(1)}, u32[]{:S(2)}, u32[]{:S(2)}) async-start(bf16[4,96,2048]{2,1,0:T(8,128)(2,1)} %bitcast.35), calls=%async_computation.4 | async-start | bytes 3145728 | tf_op jit(solution)/shard_map/all_to_all | solution.py:257
  133.6 21.6 %copy-start.1 = (bf16[1,6144,128]{2,1,0:T(8,128)(2,1)S(1)}, bf16[1,6144,128]{2,1,0:T(8,128)(2,1)}, u32[]{:S(2)}) copy-start(bf16[1,6144,128]{2,1,0:T(8,128)(2,1)} %param.25) | copy-start | bytes 4718596
  133.6 21.6 %copy-start.2 = (bf16[1,6144,128]{2,1,0:T(8,128)(2,1)S(1)}, bf16[1,6144,128]{2,1,0:T(8,128)(2,1)}, u32[]{:S(2)}) copy-start(bf16[1,6144,128]{2,1,0:T(8,128)(2,1)} %param.26) | copy-start | bytes 4718596
  181.6 27.5 %all-to-all-start.6 = ((bf16[32,20,96]{2,1,0:T(8,128)(2,1)}), bf16[32,20,96]{2,1,0:T(8,128)(2,1)S(1)}, u32[]{:S(2)}, u32[]{:S(2)}) async-start(bf16[32,20,96]{2,1,0:T(8,128)(2,1)} %bitcast.22), calls=%async_computation.6 | async-start | bytes 393216 | tf_op jit(solution)/shard_map/all_to_all | solution.py:257
